TPU v7x, 32 devices: a whole 2x2x4 slice. The times are simulated.
32 devices in a mesh: grp: 4 (over x, core), dev: 8 (over z, y).
Axes of the slice: x: 2, y: 2, z: 4, core: 2. Of those that a mesh axis runs over, the one named last changes fastest.
Arguments:
- row_ptr: int32 [4, 33], P('grp'), may hold values from 0 to 1024, as said below
- col_off: int32 [4, 1024], P('grp', 'dev'), may hold values from -24 to 24, as said below
- blocks: bfloat16 [4096, 128, 128], P(('grp', 'dev')), may hold values from -0.09375 to 0.09375
- trial: bfloat16 [16384, 256], P(('grp', 'dev')), may hold values from -6 to 6
Outputs:
- filtered: bfloat16 [24576, 256], P(('grp', 'dev'))
Inputs may be any that keep to these rules, and one draw needn't show every extreme that they name: row_ptr[g, 0] = 0 and row_ptr[g, 32] = 1024; every block row holds 24 to 48 nonzero blocks, both reached; in every band the 128 nonzero blocks of some device hold the last blocks of 6 rows. For every device d of a band, the block row that holds nonzero block d * 128 lies between (d - 1) * 4 and (d + 1) * 4. `col_off`: the offsets of one block row are distinct, increasing, and include -24, 0 and 24.
All inputs are finite; a program needn't handle non-finite values.
Results may differ from a plain program's by a relative error of at most 0.0095.
Values may be sent and summed in bfloat16 or wider, within the bound.
A program may use at most 64 MiB of HBM per device.

v0:
```python
import jax
import jax.numpy as jnp
from jax import lax
from jax.sharding import PartitionSpec as P

DEGREE = 2
SPAN = 6


filter_center = 0.5
filter_halfwidth = 1.5
piece_rows = 32
couple_floor = 24


def with_halo(block, sides, width):
    for axis, dim in sides:
        count = lax.axis_size(axis)
        forward = [(i, i + 1) for i in range(count - 1)]
        forward.append((count - 1, 0))
        backward = [(target, source) for source, target in forward]
        low = lax.ppermute(
            lax.slice_in_dim(block, block.shape[dim] - width, None, axis=dim), axis, forward
        )
        high = lax.ppermute(lax.slice_in_dim(block, 0, width, axis=dim), axis, backward)
        block = jnp.concatenate([low, block, high], axis=dim)
    return block


def from_behind(value, axis, steps):
    count = lax.axis_size(axis)
    first, last = (max(0, -steps), min(count, count - steps))
    return lax.ppermute(value, axis, [(source, source + steps) for source in range(first, last)])


def ends_before(row_ends, limits):
    return jnp.sum((row_ends[None, :] <= limits[:, None]).astype(jnp.int32), axis=1)


def extend_band(band_now, couple_rows):
    return with_halo(band_now, (("grp", 0),), couple_rows)


def local(row_ptr, col_off, blocks, trial):
    nnz_here = blocks.shape[0]
    block_rows = blocks.shape[1]
    vectors = trial.shape[1]
    pointer = row_ptr[0]
    row_ends = pointer[1:]
    band_rows = row_ends.shape[0]
    couple_rows = max(couple_floor, band_rows // 2)
    member = lax.axis_index("dev")
    first_nnz = member * nnz_here
    ordinal = first_nnz + jnp.arange(nnz_here, dtype=jnp.int32)
    row_of = ends_before(row_ends, ordinal)
    first_row = row_of[0]
    local_row = row_of - first_row
    finished = jnp.sum(
        ((row_ends > first_nnz) & (row_ends <= first_nnz + nnz_here)).astype(jnp.int32)
    )
    last_local = row_of[nnz_here - 1] - first_row
    continues = last_local == finished
    touched = SPAN + 1
    slot_ids = jnp.arange(SPAN, dtype=jnp.int32)
    filled = slot_ids < finished
    row_ids = jnp.arange(band_rows, dtype=jnp.int32)
    finisher = (row_ends - 1) // nnz_here
    finisher_first = ends_before(row_ends, finisher * nnz_here)
    source = finisher * SPAN + row_ids - finisher_first
    selector = (local_row[None, :] == jnp.arange(touched, dtype=jnp.int32)[:, None]).astype(
        jnp.float32
    )
    turns = nnz_here // piece_rows
    window_index = row_of + col_off[0] + couple_rows
    slot_index = first_row + slot_ids + couple_rows
    band_now = lax.all_gather(trial, "dev", axis=0, tiled=True).reshape(
        band_rows, block_rows, vectors
    )
    window = extend_band(band_now, couple_rows)
    earlier = window
    slot_rows = jnp.zeros((SPAN, block_rows, vectors), jnp.bfloat16)
    for degree in range(DEGREE):

        def one_turn(running, turn_index):
            offset_rows = turn_index * piece_rows
            wanted = lax.dynamic_slice_in_dim(window_index, offset_rows, piece_rows)
            matrices = lax.dynamic_slice_in_dim(blocks, offset_rows, piece_rows, 0)
            chosen = lax.dynamic_slice_in_dim(selector, offset_rows, piece_rows, 1)
            picked = jnp.take(window, wanted, axis=0)
            products = jnp.einsum(
                "pij,pjm->pim", matrices, picked, preferred_element_type=jnp.float32
            )
            return (running + jnp.einsum("tp,pim->tim", chosen, products), None)

        initial = jnp.zeros((touched, block_rows, vectors), jnp.float32)
        running = lax.scan(one_turn, initial, jnp.arange(turns, dtype=jnp.int32))[0]
        tail_row = lax.dynamic_index_in_dim(running, last_local, 0, keepdims=False)
        tail_row = jnp.where(continues, tail_row, 0.0)
        carried = from_behind(tail_row.astype(jnp.bfloat16), "dev", 1).astype(tail_row.dtype)
        row_sums = running.at[0].add(carried)[:SPAN]
        present = jnp.take(window, slot_index, axis=0, mode="clip").astype(jnp.float32)
        if degree == 0:
            updated = (row_sums - filter_center * present) / filter_halfwidth
        else:
            older = jnp.take(earlier, slot_index, axis=0, mode="clip").astype(jnp.float32)
            updated = 2.0 * (row_sums - filter_center * present) / filter_halfwidth - older
        slot_rows = jnp.where(filled[:, None, None], updated, 0.0).astype(jnp.bfloat16)
        if degree + 1 < DEGREE:
            earlier = window
            gathered = lax.all_gather(slot_rows, "dev", axis=0, tiled=True)
            band_now = jnp.take(gathered, source, axis=0)
            window = extend_band(band_now, couple_rows)
    return slot_rows.reshape(SPAN * block_rows, vectors)


def solution(mesh):
    in_specs = (
        P("grp", None),
        P("grp", "dev"),
        P(("grp", "dev"), None, None),
        P(("grp", "dev"), None),
    )
    out_specs = P(("grp", "dev"), None)
    return jax.shard_map(local, mesh=mesh, in_specs=in_specs, out_specs=out_specs, check_vma=False)
```

profile of v0, /device:TPU:27, one launch (start us, length us, event | category | flops | bytes accessed | tf_op | source)
XLA Modules:
  0.0 314.4 jit_solution(5394695339505362085)
XLA Ops:
  7.3 50.9 %all-gather.3.cloned.1.call-done = bf16[4096,256]{1,0:T(8,128)(2,1)} async-done(((bf16[512,256]{1,0:T(8,128)(2,1)}), bf16[4096,256]{1,0:T(8,128)(2,1)}) %all-gather.3.cloned.1.call-update) | async-done | bytes 2097168 | tf_op jit(solution)/shard_map/all_gather | solution.py:76
  58.2 4.0 %fusion.46 = (bf16[3072,256]{1,0:T(8,128)(2,1)}, bf16[3072,256]{1,0:T(8,128)(2,1)}) fusion(bf16[4096,256]{1,0:T(8,128)(2,1)} %all-gather.3.cloned.1.call-done), kind=kLoop, calls=%fused_computation.89 | loop fusion | bytes 6291456 | tf_op jit(solution)/shard_map/slice | solution.py:23
  62.1 0.9 collective-permute-start
  65.0 1.3 broadcast_multiply_fusion
  68.2 27.5 %collective-permute-done = bf16[24,128,256]{2,1,0:T(8,128)(2,1)} collective-permute-done((bf16[24,128,256]{2,1,0:T(8,128)(2,1)}, bf16[24,128,256]{2,1,0:T(8,128)(2,1)}, u32[]{:S(2)}, u32[]{:S(2)}) %collective-permute-start) | collective-permute-done | bytes 1572896 | tf_op jit(solution)/shard_map/ppermute | solution.py:22
  95.7 3.5 %collective-permute-done.1 = bf16[24,128,256]{2,1,0:T(8,128)(2,1)} collective-permute-done((bf16[24,128,256]{2,1,0:T(8,128)(2,1)}, bf16[24,128,256]{2,1,0:T(8,128)(2,1)}, u32[]{:S(2)}, u32[]{:S(2)}) %collective-permute-start.1) | collective-permute-done | bytes 1572896 | tf_op jit(solution)/shard_map/ppermute | solution.py:25
  99.2 4.8 %pad_maximum_fusion = bf16[80,128,256]{2,1,0:T(8,128)(2,1)} fusion(bf16[24,128,256]{2,1,0:T(8,128)(2,1)} %collective-permute-done.1, bf16[32,128,256]{2,1,0:T(8,128)(2,1)S(1)} %bitcast.61, bf16[24,128,256]{2,1,0:T(8,128)(2,1)} %collective-permute-done), kind=kLoop, calls=%fused_computation.37 | loop fusion | flops 5242880 | bytes 10485760 | tf_op jit(solution)/shard_map/concatenate | solution.py:26
  104.0 39.1 %while.24 = (s32[]{:T(128)}, f32[7,128,256]{2,0,1:T(8,128)S(1)}, s32[4]{0:T(128)S(1)}, bf16[7,128]{1,0:T(8,128)(2,1)S(1)}, bf16[128,128,128]{2,1,0:T(8,128)(2,1)...) while((s32[]{:T(128)}, f32[7,128,256]{2,0,1:T(8,128)S(1)}, ...), condition=%wide.region_4.6_spmd.clone, body=%wide.region_3.5_spmd.clone.sunk | while | flops 284624064 | bytes 13375997 | solution.py:96
  105.3 4.5 %gather_fusion = bf16[32,128,256]{2,1,0:T(8,128)(2,1)} fusion(bf16[80,128,256]{2,1,0:T(8,128)(2,1)} %get-tuple-element.326, s32[1024]{0:T(1024)S(1)} %pad_clamp_fusion.6), kind=kCustom, calls=%fused_computation.clone.clone.1 | custom fusion | bytes 4194432 | tf_op jit(solution)/shard_map/while/body/eval_jaxpr/jit(_take)/gather | solution.py:89
  109.8 2.7 fusion.64
  112.5 1.3 fusion.65
  115.0 4.5 %gather_fusion = bf16[32,128,256]{2,1,0:T(8,128)(2,1)} fusion(bf16[80,128,256]{2,1,0:T(8,128)(2,1)} %get-tuple-element.326, s32[1024]{0:T(1024)S(1)} %pad_clamp_fusion.6), kind=kCustom, calls=%fused_computation.clone.clone.1 | custom fusion | bytes 4194432 | tf_op jit(solution)/shard_map/while/body/eval_jaxpr/jit(_take)/gather | solution.py:89
  119.6 2.7 fusion.64
  122.3 1.3 fusion.65
  124.8 4.5 %gather_fusion = bf16[32,128,256]{2,1,0:T(8,128)(2,1)} fusion(bf16[80,128,256]{2,1,0:T(8,128)(2,1)} %get-tuple-element.326, s32[1024]{0:T(1024)S(1)} %pad_clamp_fusion.6), kind=kCustom, calls=%fused_computation.clone.clone.1 | custom fusion | bytes 4194432 | tf_op jit(solution)/shard_map/while/body/eval_jaxpr/jit(_take)/gather | solution.py:89
  129.3 2.7 fusion.64
  132.0 1.3 fusion.65
  134.6 4.5 %gather_fusion = bf16[32,128,256]{2,1,0:T(8,128)(2,1)} fusion(bf16[80,128,256]{2,1,0:T(8,128)(2,1)} %get-tuple-element.326, s32[1024]{0:T(1024)S(1)} %pad_clamp_fusion.6), kind=kCustom, calls=%fused_computation.clone.clone.1 | custom fusion | bytes 4194432 | tf_op jit(solution)/shard_map/while/body/eval_jaxpr/jit(_take)/gather | solution.py:89
  139.1 2.7 fusion.64
  141.8 1.3 fusion.65
  143.5 2.2 collective-permute-start.2
  146.3 3.1 gather_fusion.2
  150.1 0.9 fusion.33
  151.4 59.0 %all-gather.5.cloned.1.call-done = bf16[48,128,256]{2,1,0:T(8,128)(2,1)} async-done(((bf16[6,128,256]{2,1,0:T(8,128)(2,1)}), bf16[48,128,256]{2,1,0:T(8,128)(2,1)}) %all-gather.5.cloned.1.call-update) | async-done | bytes 3145744 | tf_op jit(solution)/shard_map/all_gather | solution.py:110
  210.4 4.0 %gather_fusion.3 = bf16[32,128,256]{2,1,0:T(8,128)(2,1)} fusion(bf16[48,128,256]{2,1,0:T(8,128)(2,1)} %all-gather.5.cloned.1.call-done, s32[1024]{0:T(1024)S(1)} %pad_clamp_fusion.2), kind=kCustom, calls=%fused_computation.3 | custom fusion | bytes 4194432 | tf_op jit(solution)/shard_map/jit(_take)/gather | solution.py:111
  214.4 1.8 broadcast_select_fusion
  216.2 2.0 fusion.45
  218.2 0.8 collective-permute-start.3
  219.0 32.7 %collective-permute-done.3 = bf16[24,128,256]{2,1,0:T(8,128)(2,1)} collective-permute-done((bf16[24,128,256]{2,1,0:T(8,128)(2,1)}, bf16[24,128,256]{2,1,0:T(8,128)(2,1)}, u32[]{:S(2)}, u32[]{:S(2)}) %collective-permute-start.3) | collective-permute-done | bytes 1572896 | tf_op jit(solution)/shard_map/ppermute | solution.py:22
  251.7 3.5 %collective-permute-done.4 = bf16[24,128,256]{2,1,0:T(8,128)(2,1)} collective-permute-done((bf16[24,128,256]{2,1,0:T(8,128)(2,1)}, bf16[24,128,256]{2,1,0:T(8,128)(2,1)}, u32[]{:S(2)}, u32[]{:S(2)}) %collective-permute-start.4) | collective-permute-done | bytes 1572896 | tf_op jit(solution)/shard_map/ppermute | solution.py:25
  255.1 4.8 %pad_maximum_fusion.1 = bf16[80,128,256]{2,1,0:T(8,128)(2,1)} fusion(bf16[24,128,256]{2,1,0:T(8,128)(2,1)} %collective-permute-done.4, bf16[32,128,256]{2,1,0:T(8,128)(2,1)S(1)} %broadcast_select_fusion, bf16[24,128,256]{2,1,0:T(8,128)(2,1)} %collective-permute-done.3), kind=kLoop, calls=%fused_computation.38 | loop fusion | flops 5242880 | bytes 10485760 | tf_op jit(solution)/shard_map/concatenate | solution.py:26
  260.0 39.7 %while.25 = (s32[]{:T(128)}, f32[7,128,256]{2,0,1:T(8,128)S(1)}, s32[4]{0:T(128)S(1)}, bf16[7,128]{1,0:T(8,128)(2,1)S(1)}, bf16[128,128,128]{2,1,0:T(8,128)(2,1)...) while((s32[]{:T(128)}, f32[7,128,256]{2,0,1:T(8,128)S(1)}, ...), condition=%wide.region_6.8_spmd.clone, body=%wide.region_5.7_spmd.clone.sunk | while | flops 284624064 | bytes 13376181 | solution.py:96
  261.3 4.5 %gather_fusion.1 = bf16[32,128,256]{2,1,0:T(8,128)(2,1)} fusion(bf16[80,128,256]{2,1,0:T(8,128)(2,1)} %get-tuple-element.359, s32[1024]{0:T(1024)S(1)} %pad_clamp_fusion.7), kind=kCustom, calls=%fused_computation.1.clone.clone.1 | custom fusion | bytes 4194432 | tf_op jit(solution)/shard_map/while/body/eval_jaxpr/jit(_take)/gather | solution.py:89
  265.8 2.7 fusion.70
  268.5 1.3 fusion.71
  271.2 4.5 %gather_fusion.1 = bf16[32,128,256]{2,1,0:T(8,128)(2,1)} fusion(bf16[80,128,256]{2,1,0:T(8,128)(2,1)} %get-tuple-element.359, s32[1024]{0:T(1024)S(1)} %pad_clamp_fusion.7), kind=kCustom, calls=%fused_computation.1.clone.clone.1 | custom fusion | bytes 4194432 | tf_op jit(solution)/shard_map/while/body/eval_jaxpr/jit(_take)/gather | solution.py:89
  275.7 2.7 fusion.70
  278.5 1.3 fusion.71
  281.2 4.5 %gather_fusion.1 = bf16[32,128,256]{2,1,0:T(8,128)(2,1)} fusion(bf16[80,128,256]{2,1,0:T(8,128)(2,1)} %get-tuple-element.359, s32[1024]{0:T(1024)S(1)} %pad_clamp_fusion.7), kind=kCustom, calls=%fused_computation.1.clone.clone.1 | custom fusion | bytes 4194432 | tf_op jit(solution)/shard_map/while/body/eval_jaxpr/jit(_take)/gather | solution.py:89
  285.7 2.7 fusion.70
  288.4 1.3 fusion.71
  291.1 4.5 %gather_fusion.1 = bf16[32,128,256]{2,1,0:T(8,128)(2,1)} fusion(bf16[80,128,256]{2,1,0:T(8,128)(2,1)} %get-tuple-element.359, s32[1024]{0:T(1024)S(1)} %pad_clamp_fusion.7), kind=kCustom, calls=%fused_computation.1.clone.clone.1 | custom fusion | bytes 4194432 | tf_op jit(solution)/shard_map/while/body/eval_jaxpr/jit(_take)/gather | solution.py:89
  295.6 2.7 fusion.70
  298.3 1.3 fusion.71
  300.0 2.2 collective-permute-start.5
  302.1 3.1 gather_fusion.4
  305.2 1.3 collective-permute-done.5
  306.6 1.0 fusion.35
  (90 shorter events, 10.7 us)
Async XLA Ops:
  6.5 51.6 %all-gather.3.cloned.1.call-start = ((), (), s32[]{:S(2)}) async-start(), calls=%async_computation | async-start | bytes 2359296 | tf_op jit(solution)/shard_map/all_gather | solution.py:76
  7.3 55.8 %copy-start.4 = (s32[1,33]{1,0:T(1,128)S(1)}, s32[1,33]{1,0:T(1,128)}, u32[]{:S(2)}) copy-start(s32[1,33]{1,0:T(1,128)} %param.14) | copy-start | bytes 400
  7.3 60.3 %copy-start.3 = (s32[1,128]{1,0:T(1,128)S(1)}, s32[1,128]{1,0:T(1,128)}, u32[]{:S(2)}) copy-start(s32[1,128]{1,0:T(1,128)} %param.15) | copy-start | bytes 1540
  7.3 203.1 %all-gather.5.cloned.1.call-start = ((), (), s32[]{:S(2)}) async-start(), calls=%async_computation.1 | async-start | bytes 3538944 | tf_op jit(solution)/shard_map/all_gather | solution.py:110
  58.2 41.0 %copy-start = (bf16[4096,256]{1,0:T(8,128)(2,1)S(1)}, bf16[4096,256]{1,0:T(8,128)(2,1)}, u32[]{:S(2)}) copy-start(bf16[4096,256]{1,0:T(8,128)(2,1)} %all-gather.3.cloned.1.call-done) | copy-start | bytes 6291460
  62.1 33.6 %collective-permute-start = (bf16[24,128,256]{2,1,0:T(8,128)(2,1)}, bf16[24,128,256]{2,1,0:T(8,128)(2,1)}, u32[]{:S(2)}, u32[]{:S(2)}) collective-permute-start(bf16[24,128,256]{2,1,0:T(8,128)(2,1)} %bitcast.3), channel_id=1, source_target_pairs={{0,8},{8,16},{16,24},{24,0},{1,9},{9,17},{17,25},{25,1},{2,10},{10... | collective-permute-start | bytes 4718600 | tf_op jit(solution)/shard_map/ppermute | solution.py:22
  63.0 36.2 %collective-permute-start.1 = (bf16[24,128,256]{2,1,0:T(8,128)(2,1)}, bf16[24,128,256]{2,1,0:T(8,128)(2,1)}, u32[]{:S(2)}, u32[]{:S(2)}) collective-permute-start(bf16[24,128,256]{2,1,0:T(8,128)(2,1)} %bitcast.5), channel_id=1, source_target_pairs={{8,0},{16,8},{24,16},{0,24},{9,1},{17,9},{25,17},{1,25},{10,2},{18... | collective-permute-start | bytes 4718600 | tf_op jit(solution)/shard_map/ppermute | solution.py:25
  63.1 40.9 %copy-start.8 = (s32[32]{0:T(128)}, s32[32]{0:T(128)S(1)}, u32[]{:S(2)}) copy-start(s32[32]{0:T(128)S(1)} %slice_bitcast_fusion) | copy-start | bytes 388
  143.4 7.7 %copy-start.7 = (s32[32]{0:T(128)S(1)}, s32[32]{0:T(128)}, u32[]{:S(2)}) copy-start(s32[32]{0:T(128)} %get-tuple-element.193) | copy-start | bytes 388
  143.4 7.7 %copy-start.9 = (s32[32]{0:T(128)S(1)}, s32[32]{0:T(128)}, u32[]{:S(2)}) copy-start(s32[32]{0:T(128)} %copy-done.8) | copy-start | bytes 388
  143.5 7.8 %copy-start.5 = (s32[1,33]{1,0:T(1,128)S(1)}, s32[1,33]{1,0:T(1,128)}, u32[]{:S(2)}) copy-start(s32[1,33]{1,0:T(1,128)} %param.14) | copy-start | bytes 400
  143.5 7.9 %copy-start.6 = (s32[32]{0:T(128)S(1)}, s32[32]{0:T(128)}, u32[]{:S(2)}) copy-start(s32[32]{0:T(128)} %get-tuple-element.194) | copy-start | bytes 388
  143.5 6.6 %collective-permute-start.2 = (bf16[128,256]{1,0:T(8,128)(2,1)S(1)}, bf16[128,256]{1,0:T(8,128)(2,1)S(1)}, u32[]{:S(2)}, u32[]{:S(2)}) collective-permute-start(bf16[128,256]{1,0:T(8,128)(2,1)S(1)} %fusion.39), channel_id=1, source_target_pairs={{0,1},{1,2},{2,3},{3,4},{4,5},{5,6},{6,7},{8,9},{9,10},{10,11},{11... | collective-permute-start | bytes 196616 | tf_op jit(solution)/shard_map/ppermute | solution.py:33
  146.3 5.0 %copy-start.1 = (pred[6]{0:T(512)(128)(4,1)}, pred[6]{0:T(512)(128)(4,1)S(1)}, u32[]{:S(2)}) copy-start(pred[6]{0:T(512)(128)(4,1)S(1)} %iota_compare_fusion.1) | copy-start | bytes 22
  218.2 33.5 %collective-permute-start.3 = (bf16[24,128,256]{2,1,0:T(8,128)(2,1)}, bf16[24,128,256]{2,1,0:T(8,128)(2,1)}, u32[]{:S(2)}, u32[]{:S(2)}) collective-permute-start(bf16[24,128,256]{2,1,0:T(8,128)(2,1)} %get-tuple-element.195), channel_id=1, source_target_pairs={{0,8},{8,16},{16,24},{24,0},{1,9},{9,17},{17,25},{25,1},{2,10},{10... | collective-permute-start | bytes 4718600 | tf_op jit(solution)/shard_map/ppermute | solution.py:22
  219.0 36.2 %collective-permute-start.4 = (bf16[24,128,256]{2,1,0:T(8,128)(2,1)}, bf16[24,128,256]{2,1,0:T(8,128)(2,1)}, u32[]{:S(2)}, u32[]{:S(2)}) collective-permute-start(bf16[24,128,256]{2,1,0:T(8,128)(2,1)} %get-tuple-element.196), channel_id=1, source_target_pairs={{8,0},{16,8},{24,16},{0,24},{9,1},{17,9},{25,17},{1,25},{10,2},{18... | collective-permute-start | bytes 4718600 | tf_op jit(solution)/shard_map/ppermute | solution.py:25
  260.0 1.3 copy-start.10
  268.5 1.3 copy-start.11
  269.9 1.3 copy-start.10
  278.4 1.3 copy-start.11
  279.8 1.3 copy-start.10
  288.4 1.3 copy-start.11
  289.7 1.3 copy-start.10
  298.3 1.3 copy-start.11
  299.6 7.0 %copy-start.2 = (pred[6]{0:T(512)(128)(4,1)S(1)}, pred[6]{0:T(512)(128)(4,1)}, u32[]{:S(2)}) copy-start(pred[6]{0:T(512)(128)(4,1)} %copy-done.1) | copy-start | bytes 22
  300.0 6.6 %collective-permute-start.5 = (bf16[128,256]{1,0:T(8,128)(2,1)S(1)}, bf16[128,256]{1,0:T(8,128)(2,1)S(1)}, u32[]{:S(2)}, u32[]{:S(2)}) collective-permute-start(bf16[128,256]{1,0:T(8,128)(2,1)S(1)} %fusion.40), channel_id=1, source_target_pairs={{0,1},{1,2},{2,3},{3,4},{4,5},{5,6},{6,7},{8,9},{9,10},{10,11},{11... | collective-permute-start | bytes 196616 | tf_op jit(solution)/shard_map/ppermute | solution.py:33
Sparse Core Ops, SparseCore 0:
  9.5 48.6 all-gather.2
  151.2 59.1 all-gather.4
where the time goes:
time: 317 us; the launch traced here: 314 us
  waiting for transfers between devices  180 us (57%)
  local copies, waits for them, and re-layouts  58.2 us (18%)
  matrix products  31.9 us (10%)
  other arithmetic  17.7 us (6%)
  between operations  15.4 us (5%)
  starting transfers between devices  6.07 us (2%)
  loops' own time  5.29 us (2%)
    ppermute x2, waiting for transfers between devices, with_halo(): lax.ppermute(lax.slice_in_dim(block, block.shape[dim] - width, None, axis...  60.2 us
    all_gather x1, waiting for transfers between devices, local(): gathered = lax.all_gather(slot_rows, 'dev', axis=0, tiled=True)  59 us
    all_gather x1, waiting for transfers between devices, local(): lax.all_gather(trial, 'dev', axis=0, tiled=True)  50.9 us
    gather x8, local copies, waits for them, and re-layouts, one_turn(): picked = jnp.take(window, wanted, axis=0)  36 us
    dot_general x8, matrix products, one_turn(): jnp.einsum('pij,pjm->pim', matrices, picked, preferred_element_type=jnp.f...  21.6 us
    dot_general x8, matrix products, one_turn(): return (running + jnp.einsum('tp,pim->tim', chosen, products), None)  10.4 us
    concatenate x2, other arithmetic, with_halo(): block = jnp.concatenate([low, block, high], axis=dim)  9.62 us
    ppermute x2, waiting for transfers between devices, with_halo(): lax.ppermute(lax.slice_in_dim(block, 0, width, axis=dim), axis, backward)  6.92 us
  transfers between devices with their start and end apart: 8, of which 8 were waited for; matrix products, arithmetic and copies ran while one was open for 3% of the time, Pallas kernels for 0%

commit v1 on v0

v1 whole, which is shorter than its diff:
```python
import functools

import jax
import jax.numpy as jnp
from jax import lax
from jax.experimental import pallas as pl
from jax.experimental.pallas import tpu as pltpu
from jax.sharding import PartitionSpec as P

SPAN = 6
CENTER = 0.5
HALFWIDTH = 1.5
FLOOR = 24
DEPTH = 8
VMEM_BYTES = 56 * 1024 * 1024
MESH = pl.DeviceIdType.MESH


def grid_of(n_dev):
    z_count = 1
    while z_count * z_count < n_dev:
        z_count *= 2
    return z_count, n_dev // z_count


def spread(mine, window, rb, n_grp, n_dev, low, high, sems):
    recv_own, recv_side, send_z, send_y, send_side, local_sem = sems
    z_count, y_count = grid_of(n_dev)
    g, d = lax.axis_index("grp"), lax.axis_index("dev")
    z, y = d // y_count, lax.rem(d, y_count)
    after = lax.rem(g + 1, n_grp)
    before = lax.rem(g + n_grp - 1, n_grp)
    sends = []

    def rows(slot, count=rb):
        return window.at[pl.ds(slot * rb, count)]

    def post(cond, src, dst, send_sem, recv_sem, target):
        def make():
            return pltpu.make_async_remote_copy(
                src_ref=src, dst_ref=dst, send_sem=send_sem, recv_sem=recv_sem, device_id=target, device_id_type=MESH
            )

        @pl.when(cond)
        def _():
            make().start()

        sends.append((cond, make))

    def held(s, own):
        return mine if own else rows(n_dev + s)

    def to_sides(cond, s, own):
        src = held(s, own)
        post(cond & (s >= d + n_dev - low), src, rows(s), send_side.at[0, s], recv_side.at[0, s], (after, d))
        post(
            cond & (s <= d + high - 1 - n_dev), src, rows(2 * n_dev + s),
            send_side.at[1, s], recv_side.at[1, s], (before, d),
        )
        post(
            cond & (s == d + high - n_dev), src.at[pl.ds(0, 1)], rows(2 * n_dev + s, 1),
            send_side.at[1, s], recv_side.at[1, s], (before, d),
        )

    def arrived(cond, s):
        @pl.when(cond)
        def _():
            pltpu.make_async_copy(rows(n_dev + s), rows(n_dev + s), recv_own.at[s]).wait()

    def line_step(cond, s, way, own):
        src = held(s, own)
        if way >= 0:
            post(cond & (z < z_count - 1), src, rows(n_dev + s), send_z.at[0, s], recv_own.at[s], (g, d + y_count))
        if way <= 0:
            post(cond & (z > 0), src, rows(n_dev + s), send_z.at[1, s], recv_own.at[s], (g, d - y_count))
        for step in range(1, y_count):
            other = z * y_count + lax.rem(y + step, y_count)
            post(cond, src, rows(n_dev + s), send_y.at[step - 1, s], recv_own.at[s], (g, other))
        to_sides(cond, s, own)

    def around(k):
        if k == 0:
            return [(z >= 0, z, 0)]
        return [(z - k >= 0, z - k, 1), (z + k < z_count, z + k, -1)]

    keep = pltpu.make_async_copy(mine, rows(n_dev + d), local_sem)
    keep.start()

    def across(k):
        for cond, at, _ in around(k):
            at = jnp.clip(at, 0, z_count - 1)
            for step in range(1, y_count):
                s = at * y_count + lax.rem(y + step, y_count)
                arrived(cond, s)
                to_sides(cond, s, False)

    for k in range(z_count):
        for cond, at, way in around(k):
            s = jnp.clip(at, 0, z_count - 1) * y_count + y
            if k > 0:
                arrived(cond, s)
            line_step(cond, s, way, k == 0)
        if k > 0:
            across(k - 1)
    across(z_count - 1)

    for s in range(n_dev):
        @pl.when(s >= d + n_dev - low)
        def _(s=s):
            pltpu.make_async_copy(rows(s), rows(s), recv_side.at[0, s]).wait()

        @pl.when(s <= d + high - 1 - n_dev)
        def _(s=s):
            slot = 2 * n_dev + s
            pltpu.make_async_copy(rows(slot), rows(slot), recv_side.at[1, s]).wait()

        @pl.when(s == d + high - n_dev)
        def _(s=s):
            slot = 2 * n_dev + s
            pltpu.make_async_copy(rows(slot, 1), rows(slot, 1), recv_side.at[1, s]).wait()

    for cond, make in sends:
        @pl.when(cond)
        def _(make=make):
            make().wait_send()
    keep.wait()


def greet(n_grp, n_dev, partials):
    _, y_count = grid_of(n_dev)
    z_count = n_dev // y_count
    g, d = lax.axis_index("grp"), lax.axis_index("dev")
    z, y = d // y_count, lax.rem(d, y_count)
    barrier = pltpu.get_barrier_semaphore()
    expected = jnp.int32(0)
    targets = [
        (z >= 0, (lax.rem(g + 1, n_grp), d)),
        (z >= 0, (lax.rem(g + n_grp - 1, n_grp), d)),
        (z < z_count - 1, (g, d + y_count)),
        (z > 0, (g, d - y_count)),
    ]
    for step in range(1, y_count):
        targets.append((z >= 0, (g, z * y_count + lax.rem(y + step, y_count))))
    if partials:
        for by in (1, 2):
            targets.append((d + by < n_dev, (g, d + by)))
            targets.append((d - by >= 0, (g, d - by)))
    for cond, target in targets:
        @pl.when(cond)
        def _(target=target):
            pl.semaphore_signal(barrier, inc=1, device_id=target, device_id_type=MESH)

        expected = expected + jnp.where(cond, 1, 0)
    pl.semaphore_wait(barrier, expected)


def first_kernel(sizes, trial, window, *sems):
    rb, n_grp, n_dev, low, high = sizes
    greet(n_grp, n_dev, False)
    spread(trial, window, rb, n_grp, n_dev, low, high, sems)


def second_kernel(sizes, left, own, right, trial, window, mine, from_low, from_high, from_far, part_send, part_recv, *sems):
    rb, n_grp, n_dev, low, high = sizes
    greet(n_grp, n_dev, True)
    g, d = lax.axis_index("grp"), lax.axis_index("dev")
    parts = [
        (d < n_dev - 1, d > 0, right.at[pl.ds(0, rb)], from_low, (g, d + 1)),
        (d > 0, d < n_dev - 1, left, from_high, (g, d - 1)),
        (d < n_dev - 2, d > 1, right.at[pl.ds(rb, 1)], from_far, (g, d + 2)),
    ]

    def make(at):
        _, _, src, dst, target = parts[at]
        return pltpu.make_async_remote_copy(
            src_ref=src, dst_ref=dst, send_sem=part_send.at[at], recv_sem=part_recv.at[at],
            device_id=target, device_id_type=MESH,
        )

    for at in range(3):
        @pl.when(parts[at][0])
        def _(at=at):
            make(at).start()
    for at in range(3):
        @pl.when(parts[at][1])
        def _(at=at):
            make(at).wait_recv()
            dst = parts[at][3]
            for row in range(dst.shape[0]):
                own[row] = own[row] + dst[row].astype(jnp.float32)

    for row in range(rb):
        present = trial[row].astype(jnp.float32)
        mine[row] = ((own[row] - CENTER * present) / HALFWIDTH).astype(mine.dtype)
    spread(mine, window, rb, n_grp, n_dev, low, high, sems)
    for at in range(3):
        @pl.when(parts[at][0])
        def _(at=at):
            make(at).wait_send()


def row_sum(starts, ends, columns, blocks, window, at):
    begin, end = starts[at], ends[at]

    def step(i, total):
        lhs, rhs = [], []
        for j in range(DEPTH):
            b = begin + i * DEPTH + j
            valid = b < end
            b = jnp.minimum(b, end - 1)
            block = blocks[b]
            lhs.append(jnp.where(valid, block, jnp.zeros_like(block)))
            rhs.append(window[columns[b]])
        return total + jnp.dot(
            jnp.concatenate(lhs, axis=1), jnp.concatenate(rhs, axis=0), preferred_element_type=jnp.float32
        )

    turns = (end - begin + DEPTH - 1) // DEPTH
    return lax.fori_loop(0, turns, step, jnp.zeros(window.shape[1:], jnp.float32))


def frame_kernel(rb, starts, ends, columns, blocks, window, left, own, right):
    @pl.loop(0, rb)
    def _(row):
        left[row] = row_sum(starts, ends, columns, blocks, window, row).astype(left.dtype)

    @pl.loop(0, rb)
    def _(row):
        own[row] = row_sum(starts, ends, columns, blocks, window, rb + row)

    @pl.loop(0, rb + 1)
    def _(row):
        right[row] = row_sum(starts, ends, columns, blocks, window, 2 * rb + row).astype(right.dtype)


def slots_kernel(starts, ends, columns, places, blocks, window, older, updated, tail):
    tail[0] = row_sum(starts, ends, columns, blocks, window, SPAN).astype(tail.dtype)

    @pl.loop(0, SPAN)
    def _(slot):
        total = row_sum(starts, ends, columns, blocks, window, slot)
        present = window[places[0] + slot].astype(jnp.float32)
        value = 2.0 * (total - CENTER * present) / HALFWIDTH - older[slot].astype(jnp.float32)
        updated[slot] = jnp.where(slot < places[1], value, jnp.zeros_like(value))


def local(n_grp, n_dev, row_ptr, col_off, blocks, trial):
    nnz_here, blk, _ = blocks.shape
    vectors = trial.shape[1]
    pointer = row_ptr[0]
    row_ends = pointer[1:]
    band_rows = row_ends.shape[0]
    rb = band_rows // n_dev
    half = max(FLOOR, band_rows // 2)
    reach = -(-half // rb)
    low, high = 1 + reach, 2 + reach
    z_count, y_count = grid_of(n_dev)
    member = lax.axis_index("dev")
    first_nnz = member * nnz_here

    ordinal = first_nnz + jnp.arange(nnz_here, dtype=jnp.int32)
    row_of = jnp.sum((row_ends[None, :] <= ordinal[:, None]).astype(jnp.int32), axis=1)
    columns = (row_of + col_off[0] + band_rows).astype(jnp.int32)
    first_row = row_of[0]
    finished = jnp.sum(((row_ends > first_nnz) & (row_ends <= first_nnz + nnz_here)).astype(jnp.int32))

    def segments(row_ids):
        inside = (row_ids >= 0) & (row_ids < band_rows)
        safe = jnp.clip(row_ids, 0, band_rows - 1)
        begin = jnp.clip(pointer[safe] - first_nnz, 0, nnz_here)
        end = jnp.clip(row_ends[safe] - first_nnz, 0, nnz_here)
        return jnp.where(inside, begin, 0), jnp.where(inside, end, 0)

    frame_starts, frame_ends = segments((member - 1) * rb + jnp.arange(3 * rb + 1, dtype=jnp.int32))
    slot_ids = jnp.arange(SPAN + 1, dtype=jnp.int32)
    tail_row = first_row + finished
    slot_starts, slot_ends = segments(jnp.where(slot_ids < SPAN, first_row + slot_ids, tail_row))
    slot_ends = jnp.where((slot_ids < finished) | (slot_ids == SPAN), slot_ends, slot_starts)
    places = jnp.stack([first_row + band_rows, finished]).astype(jnp.int32)

    own_rows = trial.reshape(rb, blk, vectors)
    sizes = (rb, n_grp, n_dev, low, high)
    dma = pltpu.SemaphoreType.DMA
    sems = [
        dma((n_dev,)), dma((2, n_dev)), dma((2, n_dev)), dma((max(1, y_count - 1), n_dev)), dma((2, n_dev)), dma,
    ]
    any_spec = pl.BlockSpec(memory_space=pl.ANY)
    vmem = pl.BlockSpec(memory_space=pltpu.VMEM)
    smem = pl.BlockSpec(memory_space=pltpu.SMEM)
    kept = trial.dtype

    def shape(rows, dtype):
        return jax.ShapeDtypeStruct((rows, blk, vectors), dtype)

    def remote(collective_id):
        return pltpu.CompilerParams(
            collective_id=collective_id, has_side_effects=True, vmem_limit_bytes=VMEM_BYTES
        )

    here = pltpu.CompilerParams(vmem_limit_bytes=VMEM_BYTES)
    window = pl.pallas_call(
        functools.partial(first_kernel, sizes),
        out_shape=shape(3 * band_rows, kept),
        in_specs=[any_spec],
        out_specs=any_spec,
        scratch_shapes=sems,
        compiler_params=remote(0),
        name="spread_trial",
    )(own_rows)
    left, own, right = pl.pallas_call(
        functools.partial(frame_kernel, rb),
        out_shape=(shape(rb, kept), shape(rb, jnp.float32), shape(rb + 1, kept)),
        in_specs=[smem] * 3 + [vmem] * 2,
        out_specs=(vmem, vmem, vmem),
        compiler_params=here,
        name="sums_first",
    )(frame_starts, frame_ends, columns, blocks, window)
    older = lax.dynamic_slice_in_dim(window, places[0], SPAN, 0)

    def after_parts(left, own, right, trial, window, total, *rest):
        for row in range(rb):
            total[row] = own[row]
        second_kernel(sizes, left, total, right, trial, window, *rest)

    window = pl.pallas_call(
        after_parts,
        out_shape=shape(3 * band_rows, kept),
        in_specs=[vmem] * 4,
        out_specs=any_spec,
        scratch_shapes=[
            pltpu.VMEM((rb, blk, vectors), jnp.float32),
            pltpu.VMEM((rb, blk, vectors), kept),
            pltpu.VMEM((rb, blk, vectors), kept),
            pltpu.VMEM((rb, blk, vectors), kept),
            pltpu.VMEM((1, blk, vectors), kept),
            dma((3,)),
            dma((3,)),
        ] + sems,
        compiler_params=remote(1),
        name="finish_and_spread",
    )(left, own, right, own_rows)
    updated, tail = pl.pallas_call(
        slots_kernel,
        out_shape=(shape(SPAN, jnp.float32), shape(1, kept)),
        in_specs=[smem] * 4 + [vmem] * 3,
        out_specs=(vmem, vmem),
        compiler_params=here,
        name="sums_second",
    )(slot_starts, slot_ends, columns, places, blocks, window, older)
    carried = lax.ppermute(tail, "dev", [(i, i + 1) for i in range(n_dev - 1)])
    carried = carried.astype(jnp.float32) * (2.0 / HALFWIDTH)
    first_slot = (slot_ids[:SPAN] == 0)[:, None, None]
    result = updated + jnp.where(first_slot, carried, 0.0)
    return result.astype(kept).reshape(SPAN * blk, vectors)


def solution(mesh):
    in_specs = (
        P("grp", None),
        P("grp", "dev"),
        P(("grp", "dev"), None, None),
        P(("grp", "dev"), None),
    )
    step = functools.partial(local, mesh.shape["grp"], mesh.shape["dev"])
    return jax.shard_map(step, mesh=mesh, in_specs=in_specs, out_specs=P(("grp", "dev"), None), check_vma=False)
```

time: 317 us -> 127 us (0.40)
  waiting for transfers between devices: 180 us -> 4.17 us
  Pallas kernels: 0 us -> 105 us
  local copies, waits for them, and re-layouts: 58.2 us -> 6.43 us
  matrix products: 31.9 us -> 0 us
  between operations: 15.4 us -> 0.86 us
  other arithmetic: 17.7 us -> 7.83 us
  loops' own time: 5.29 us -> 0 us
  starting transfers between devices: 6.07 us -> 1.91 us
    all_gather x2 -> x0, waiting for transfers between devices: 110 us -> none  [the longest x1 59 us: local(): gathered = lax.all_gather(slot_rows, 'dev', axis=0, tiled=True)]
    pallas_call x0 -> x4, Pallas kernels: none -> 105 us  [the longest x1 50.7 us: local(): pl.pallas_call(after_parts, out_shape=shape(3 * band_rows, kept), in_spec...]
    ppermute x6 -> x1, waiting for transfers between devices: 69.2 us -> 4.17 us  [local(): carried = lax.ppermute(tail, 'dev', [(i, i + 1) for i in range(n_dev - 1)])]
    gather x11 -> x4, local copies, waits for them, and re-layouts: 46.1 us -> 3.93 us  [the longest x2 2.62 us: segments(): begin = jnp.clip(pointer[safe] - first_nnz, 0, nnz_here)]
    dot_general x16 -> x0, matrix products: 31.9 us -> none  [the longest x8 21.6 us: one_turn(): jnp.einsum('pij,pjm->pim', matrices, picked, preferred_element_type=jnp.f...]
    concatenate x2 -> x0, other arithmetic: 9.62 us -> none  [with_halo(): block = jnp.concatenate([low, block, high], axis=dim)]
    slice x4 -> x0, local copies, waits for them, and re-layouts: 6.62 us -> none  [the longest x2 5.97 us: with_halo(): lax.slice_in_dim(block, block.shape[dim] - width, None, axis=dim)]
    another operation x2 -> x0, loops' own time: 5.29 us -> none  [local(): running = lax.scan(one_turn, initial, jnp.arange(turns, dtype=jnp.int32))[0]]
  transfers between devices with their start and end apart: 8 -> 1, of which waited for: 8 -> 1; matrix products, arithmetic and copies ran while one was open for 3% -> 0% of each run, Pallas kernels for 0% -> 0%
where the time goes in v1:
time: 127 us; the launch traced here: 126 us
  Pallas kernels  105 us (83%)
  other arithmetic  7.83 us (6%)
  local copies, waits for them, and re-layouts  6.43 us (5%)
  waiting for transfers between devices  4.17 us (3%)
  starting transfers between devices  1.91 us (2%)
    pallas_call x1, Pallas kernels, local(): pl.pallas_call(after_parts, out_shape=shape(3 * band_rows, kept), in_spec...  50.7 us
    pallas_call x1, Pallas kernels, local(): pl.pallas_call(functools.partial(first_kernel, sizes), out_shape=shape(3...  34.4 us
    pallas_call x1, Pallas kernels, local(): pl.pallas_call(functools.partial(frame_kernel, rb), out_shape=(shape(rb,...  10.1 us
    pallas_call x1, Pallas kernels, local(): pl.pallas_call(slots_kernel, out_shape=(shape(SPAN, jnp.float32), shape(1...  9.94 us
    ppermute x1, waiting for transfers between devices, local(): carried = lax.ppermute(tail, 'dev', [(i, i + 1) for i in range(n_dev - 1)])  4.17 us
    gather x2, local copies, waits for them, and re-layouts, segments(): begin = jnp.clip(pointer[safe] - first_nnz, 0, nnz_here)  2.62 us
  transfers between devices with their start and end apart: 1, of which 1 were waited for; matrix products, arithmetic and copies ran while one was open for 0% of the time, Pallas kernels for 0%

profile of v1, /device:TPU:27, one launch (start us, length us, event | category | flops | bytes accessed | tf_op | source)
XLA Modules:
  0.0 126.3 jit_solution(13725387273956640768)
XLA Ops:
  0.0 0.7 slice_bitcast_fusion
  0.8 1.4 %fusion = s32[]{:T(128)} fusion(s32[]{:T(128)S(6)} %add.123, s32[]{:T(128)S(6)} %mul.12, s32[1,33]{1,0:T(1,128)} %param.4), kind=kLoop, calls=%fused_computation.21 | loop fusion | flops 159 | bytes 140 | tf_op jit(solution)/shard_map/reduce_sum | solution.py:265
  2.1 0.1 convert_reduce_fusion
  3.0 1.2 fusion.6.columns
  4.2 0.7 gather_fusion.3
  4.9 1.3 %gather_fusion = s32[7]{0:T(128)S(1)} fusion(s32[33]{0:T(128)} %bitcast.25, s32[1024]{0:T(1024)S(1)} %pad_clamp_fusion.3), kind=kCustom, calls=%fused_computation | custom fusion | bytes 84 | tf_op jit(solution)/shard_map/gather | solution.py:270
  6.2 1.3 %gather_fusion.2 = s32[13]{0:T(128)S(1)} fusion(s32[33]{0:T(128)} %bitcast.26, s32[1024]{0:T(1024)S(1)} %pad_clamp_fusion.1), kind=kCustom, calls=%fused_computation.2 | custom fusion | bytes 156 | tf_op jit(solution)/shard_map/gather | solution.py:270
  7.5 0.6 gather_fusion.1
  8.2 34.4 %spread_trial.1.window = bf16[96,128,256]{2,1,0:T(8,128)(2,1)} custom-call(bf16[4,128,256]{2,1,0:T(8,128)(2,1)} %bitcast.27), custom_call_target="tpu_custom_call" | custom-call | tf_op jit(solution)/shard_map/spread_trial/pallas_call | solution.py:301
  42.6 1.2 pad_add_fusion.places
  43.8 0.6 clamp_select_fusion
  44.4 1.2 or_select_fusion
  45.6 1.8 %constant_dynamic-slice_fusion.older = bf16[6,128,256]{2,1,0:T(8,128)(2,1)} fusion(bf16[96,128,256]{2,1,0:T(8,128)(2,1)} %spread_trial.1.window, s32[]{:T(128)S(6)} %select_n.93), kind=kLoop, calls=%fused_computation.37 | loop fusion | bytes 786436 | tf_op jit(solution)/shard_map/dynamic_slice | solution.py:318
  47.4 10.1 %sums_first.1 = (bf16[4,128,256]{2,1,0:T(8,128)(2,1)}, f32[4,128,256]{2,1,0:T(8,128)}, bf16[5,128,256]{2,1,0:T(8,128)(2,1)}) custom-call(s32[13]{0:T(128)} %get-tuple-element.18.starts, s32[13]{0:T(128)} %get-tuple-element.17.ends, s32[128]{0:T(128)} %fusion.6.columns, bf16[128,128,128]{2,1,0:T(8,128)(2,1)} %blocks.3, bf16[96,128,256]{2,1,0:T(8,128)(2,1)} %spread_trial.1.window), custom_call_target="tpu_custom_call" | custom-call | tf_op jit(solution)/shard_map/sums_first/pallas_call | solution.py:310
  57.5 50.7 %finish_and_spread.1.window = bf16[96,128,256]{2,1,0:T(8,128)(2,1)} custom-call(bf16[4,128,256]{2,1,0:T(8,128)(2,1)} %get-tuple-element.10.left, f32[4,128,256]{2,1,0:T(8,128)} %get-tuple-element.11.own, bf16[5,128,256]{2,1,0:T(8,128)(2,1)} %get-tuple-element.12.right, bf16[4,128,256]{2,1,0:T(8,128)(2,1)} %bitcast.28), custom_call_target="tpu_custom_call" | custom-call | tf_op jit(solution)/shard_map/finish_and_spread/pallas_call | solution.py:325
  108.2 9.9 %sums_second.1 = (f32[6,128,256]{2,1,0:T(8,128)}, bf16[1,128,256]{2,1,0:T(8,128)(2,1)}) custom-call(s32[7]{0:T(128)} %get-tuple-element.16.starts, s32[7]{0:T(128)} %get-tuple-element.15.ends, s32[128]{0:T(128)} %fusion.6.columns, s32[2]{0:T(128)} %pad_add_fusion.places, bf16[128,128,128]{2,1,0:T(8,128)(2,1)} %blocks.3, ...), custom_call_target="tpu_custom_call" | custom-call | tf_op jit(solution)/shard_map/sums_second/pallas_call | solution.py:342
  118.1 1.9 %collective-permute-start = (bf16[1,128,256]{2,1,0:T(8,128)(2,1)}, bf16[1,128,256]{2,1,0:T(8,128)(2,1)S(1)}, u32[]{:S(2)}, u32[]{:S(2)}) collective-permute-start(bf16[1,128,256]{2,1,0:T(8,128)(2,1)} %get-tuple-element.14), channel_id=1, source_target_pairs={{0,1},{1,2},{2,3},{3,4},{4,5},{5,6},{6,7},{8,9},{9,10},{10,11},{11... | collective-permute-start | bytes 196616 | tf_op jit(solution)/shard_map/ppermute | solution.py:350
  120.0 4.2 %collective-permute-done = bf16[1,128,256]{2,1,0:T(8,128)(2,1)S(1)} collective-permute-done((bf16[1,128,256]{2,1,0:T(8,128)(2,1)}, bf16[1,128,256]{2,1,0:T(8,128)(2,1)S(1)}, u32[]{:S(2)}, u32[]{:S(2)}) %collective-permute-start) | collective-permute-done | bytes 65568 | tf_op jit(solution)/shard_map/ppermute | solution.py:350
  124.2 2.0 %add_convert_fusion = bf16[6,128,256]{2,1,0:T(8,128)(2,1)} fusion(f32[6,128,256]{2,1,0:T(8,128)} %get-tuple-element.13, f32[128,256]{1,0:T(8,128)S(1)} %multiply_bitcast_fusion, pred[6]{0:T(512)(128)(4,1)S(1)} %slice_compare_fusion), kind=kLoop, calls=%fused_computation.4 | loop fusion | flops 589824 | bytes 1310726 | tf_op jit(solution)/shard_map/convert_element_type | solution.py:354
  (11 shorter events, 0.1 us)
Async XLA Ops:
  118.1 6.1 %collective-permute-start = (bf16[1,128,256]{2,1,0:T(8,128)(2,1)}, bf16[1,128,256]{2,1,0:T(8,128)(2,1)S(1)}, u32[]{:S(2)}, u32[]{:S(2)}) collective-permute-start(bf16[1,128,256]{2,1,0:T(8,128)(2,1)} %get-tuple-element.14), channel_id=1, source_target_pairs={{0,1},{1,2},{2,3},{3,4},{4,5},{5,6},{6,7},{8,9},{9,10},{10,11},{11... | collective-permute-start | bytes 196616 | tf_op jit(solution)/shard_map/ppermute | solution.py:350

commit v2 on v1

v2 whole, which is shorter than its diff:
```python
import functools

import jax
import jax.numpy as jnp
from jax import lax
from jax.experimental import pallas as pl
from jax.experimental.pallas import tpu as pltpu
from jax.sharding import PartitionSpec as P

SPAN = 6
CENTER = 0.5
HALFWIDTH = 1.5
FLOOR = 24
DEPTH = 16
CHUNKS = 4
VMEM_BYTES = 56 * 1024 * 1024
MESH = pl.DeviceIdType.MESH


def grid_of(n_dev):
    z_count = 1
    while z_count * z_count < n_dev:
        z_count *= 2
    return z_count, n_dev // z_count


def spread(mine, window, rb, n_grp, n_dev, low, high, sems, prepare=None):
    recv_own, recv_side, send_z, send_y, send_side, local_sem = sems
    z_count, y_count = grid_of(n_dev)
    g, d = lax.axis_index("grp"), lax.axis_index("dev")
    z, y = d // y_count, lax.rem(d, y_count)
    after = lax.rem(g + 1, n_grp)
    before = lax.rem(g + n_grp - 1, n_grp)
    sends = []

    def rows(slot, p=None, count=1):
        return window.at[pl.ds(slot * rb, rb)] if p is None else window.at[pl.ds(slot * rb + p, count)]

    def post(cond, src, dst, send_sem, recv_sem, target):
        @pl.when(cond)
        def _():
            pltpu.make_async_remote_copy(
                src_ref=src, dst_ref=dst, send_sem=send_sem, recv_sem=recv_sem, device_id=target, device_id_type=MESH
            ).start()

    def drain(cond, ref, sem):
        @pl.when(cond)
        def _():
            pltpu.make_async_copy(ref, ref, sem).wait()

    def to_sides(cond, s, p, src):
        post(cond & (s >= d + n_dev - low), src, rows(s, p), send_side.at[0, s], recv_side.at[0, s], (after, d))
        post(
            cond & ((s <= d + high - 1 - n_dev) | ((s == d + high - n_dev) & (p == 0))), src, rows(2 * n_dev + s, p),
            send_side.at[1, s], recv_side.at[1, s], (before, d),
        )

    def line_step(cond, s, p, way, src):
        dst = rows(n_dev + s, p)
        if way >= 0:
            post(cond & (z < z_count - 1), src, dst, send_z.at[0, s], recv_own.at[s, p], (g, d + y_count))
        if way <= 0:
            post(cond & (z > 0), src, dst, send_z.at[1, s], recv_own.at[s, p], (g, d - y_count))
        for step in range(1, y_count):
            other = z * y_count + lax.rem(y + step, y_count)
            post(cond, src, dst, send_y.at[step - 1, s], recv_own.at[s, p], (g, other))
        to_sides(cond, s, p, src)

    def around(k):
        if k == 0:
            return [(z >= 0, z, 0)]
        return [(z - k >= 0, z - k, 1), (z + k < z_count, z + k, -1)]

    def across(k, p):
        for cond, at, _ in around(k):
            at = jnp.clip(at, 0, z_count - 1)
            for step in range(1, y_count):
                s = at * y_count + lax.rem(y + step, y_count)
                drain(cond, rows(n_dev + s, p), recv_own.at[s, p])
                to_sides(cond, s, p, rows(n_dev + s, p))

    @pl.loop(0, rb)
    def _(p):
        if prepare is not None:
            prepare(p)
        line_step(z >= 0, d, p, 0, mine.at[pl.ds(p, 1)])

    keep = pltpu.make_async_copy(mine, rows(n_dev + d), local_sem)
    keep.start()

    for k in range(1, z_count + 1):
        @pl.loop(0, rb)
        def _(p, k=k):
            if k < z_count:
                for cond, at, way in around(k):
                    s = jnp.clip(at, 0, z_count - 1) * y_count + y
                    drain(cond, rows(n_dev + s, p), recv_own.at[s, p])
                    line_step(cond, s, p, way, rows(n_dev + s, p))
            across(k - 1, p)

    @pl.loop(0, n_dev)
    def _(s):
        s_z, s_y = s // y_count, lax.rem(s, y_count)
        low_in, high_in, edge_in = s >= d + n_dev - low, s <= d + high - 1 - n_dev, s == d + high - n_dev
        shard, later = rows(s), rows(2 * n_dev + s)
        one = rows(2 * n_dev + s, 0)
        drain(low_in, shard, recv_side.at[0, s])
        drain(high_in, later, recv_side.at[1, s])
        drain(edge_in, one, recv_side.at[1, s])
        drain(low_in, shard, send_side.at[0, s])
        drain(high_in, later, send_side.at[1, s])
        drain(edge_in, one, send_side.at[1, s])
        mine_line = s_y == y
        drain(mine_line & (s_z <= z) & (z < z_count - 1), shard, send_z.at[0, s])
        drain(mine_line & (s_z >= z) & (z > 0), shard, send_z.at[1, s])
        for step in range(1, y_count):
            drain(mine_line, shard, send_y.at[step - 1, s])

    keep.wait()


def greet(n_grp, n_dev, partials):
    _, y_count = grid_of(n_dev)
    z_count = n_dev // y_count
    g, d = lax.axis_index("grp"), lax.axis_index("dev")
    z, y = d // y_count, lax.rem(d, y_count)
    barrier = pltpu.get_barrier_semaphore()
    expected = jnp.int32(0)
    targets = [
        (z >= 0, (lax.rem(g + 1, n_grp), d)),
        (z >= 0, (lax.rem(g + n_grp - 1, n_grp), d)),
        (z < z_count - 1, (g, d + y_count)),
        (z > 0, (g, d - y_count)),
    ]
    for step in range(1, y_count):
        targets.append((z >= 0, (g, z * y_count + lax.rem(y + step, y_count))))
    if partials:
        for by in (1, 2):
            targets.append((d + by < n_dev, (g, d + by)))
            targets.append((d - by >= 0, (g, d - by)))
    for cond, target in targets:
        @pl.when(cond)
        def _(target=target):
            pl.semaphore_signal(barrier, inc=1, device_id=target, device_id_type=MESH)

        expected = expected + jnp.where(cond, 1, 0)
    pl.semaphore_wait(barrier, expected)


def first_kernel(sizes, trial, window, *sems):
    rb, n_grp, n_dev, low, high = sizes
    greet(n_grp, n_dev, False)
    spread(trial, window, rb, n_grp, n_dev, low, high, sems)


def second_kernel(sizes, left, own, right, trial, window, mine, from_low, from_high, from_far, part_send, part_recv, *sems):
    rb, n_grp, n_dev, low, high = sizes
    greet(n_grp, n_dev, True)
    g, d = lax.axis_index("grp"), lax.axis_index("dev")
    up, down, far = (d < n_dev - 1, d > 0), (d > 0, d < n_dev - 1), (d < n_dev - 2, d > 1)

    def copy(src, dst, at, p, target):
        return pltpu.make_async_remote_copy(
            src_ref=src.at[pl.ds(p if at < 2 else rb, 1)], dst_ref=dst.at[pl.ds(p, 1)],
            send_sem=part_send.at[at, p], recv_sem=part_recv.at[at, p], device_id=target, device_id_type=MESH,
        )

    def to_up(p):
        return copy(right, from_low, 0, p, (g, d + 1))

    def to_down(p):
        return copy(left, from_high, 1, p, (g, d - 1))

    def to_far():
        return copy(right, from_far, 2, 0, (g, d + 2))

    pl.when(far[0])(lambda: to_far().start())

    @pl.loop(0, rb)
    def _(p):
        pl.when(up[0])(lambda: to_up(p).start())
        pl.when(down[0])(lambda: to_down(p).start())

    def prepare(p):
        mine_sum[p] = own[p]

        @pl.when(up[1])
        def _():
            to_up(p).wait_recv()
            mine_sum[p] = mine_sum[p] + from_low[p].astype(jnp.float32)

        @pl.when(down[1])
        def _():
            to_down(p).wait_recv()
            mine_sum[p] = mine_sum[p] + from_high[p].astype(jnp.float32)

        @pl.when(far[1] & (p == 0))
        def _():
            to_far().wait_recv()
            mine_sum[p] = mine_sum[p] + from_far[0].astype(jnp.float32)

        present = trial[p].astype(jnp.float32)
        mine[p] = ((mine_sum[p] - CENTER * present) / HALFWIDTH).astype(mine.dtype)

    mine_sum, sems = sems[0], sems[1:]
    spread(mine, window, rb, n_grp, n_dev, low, high, sems, prepare)

    @pl.loop(0, rb)
    def _(p):
        pl.when(up[0])(lambda: to_up(p).wait_send())
        pl.when(down[0])(lambda: to_down(p).wait_send())

    pl.when(far[0])(lambda: to_far().wait_send())


def fetch(sizes, blocks, window, held, near, sems):
    rb, n_grp, n_dev, low, high = sizes
    d = lax.axis_index("dev")
    base = (n_dev + d - low) * rb
    rows = pltpu.make_async_copy(window.at[pl.ds(base, near.shape[0])], near, sems.at[CHUNKS])
    rows.start()
    size = blocks.shape[0] // CHUNKS

    def part(c):
        here = pl.ds(c * size, size)
        return pltpu.make_async_copy(blocks.at[here], held.at[here], sems.at[c])

    for c in range(CHUNKS):
        part(c).start()
    rows.wait()

    def ready(begin, end):
        for c in range(CHUNKS):
            pl.when((begin <= c * size) & (end > c * size))(lambda: part(c).wait())

    return base, ready


def bounds(pointer, row, first_nnz, nnz_here):
    count = pointer.shape[1] - 1
    at = jnp.clip(row, 0, count - 1)
    begin = jnp.clip(pointer[0, at] - first_nnz, 0, nnz_here)
    end = jnp.clip(pointer[0, at + 1] - first_nnz, 0, nnz_here)
    return begin, jnp.where((row >= 0) & (row < count), end, begin)


def row_sum(begin, end, shift, offsets, held, near):
    def step(i, total):
        lhs, rhs = [], []
        for j in range(DEPTH):
            b = begin + i * DEPTH + j
            valid = b < end
            b = jnp.minimum(b, end - 1)
            block = held[b]
            lhs.append(jnp.where(valid, block, jnp.zeros_like(block)))
            rhs.append(near[offsets[0, b] + shift])
        return total + jnp.dot(
            jnp.concatenate(lhs, axis=1), jnp.concatenate(rhs, axis=0), preferred_element_type=jnp.float32
        )

    turns = (end - begin + DEPTH - 1) // DEPTH
    return lax.fori_loop(0, turns, step, jnp.zeros(near.shape[1:], jnp.float32))


def frame_kernel(sizes, pointer, offsets, blocks, window, left, own, right, held, near, sems):
    rb, n_grp, n_dev, low, high = sizes
    nnz_here = blocks.shape[0]
    d = lax.axis_index("dev")
    base, ready = fetch(sizes, blocks, window, held, near, sems)

    def one(at):
        row = (d - 1) * rb + at
        begin, end = bounds(pointer, row, d * nnz_here, nnz_here)
        ready(begin, end)
        return row_sum(begin, end, row + n_dev * rb - base, offsets, held, near)

    @pl.loop(0, rb)
    def _(at):
        left[at] = one(at).astype(left.dtype)

    @pl.loop(0, rb)
    def _(at):
        own[at] = one(rb + at)

    @pl.loop(0, rb + 1)
    def _(at):
        right[at] = one(2 * rb + at).astype(right.dtype)


def slots_kernel(sizes, pointer, offsets, blocks, window, before, filtered, head, tail, held, near, older, sems):
    rb, n_grp, n_dev, low, high = sizes
    nnz_here = blocks.shape[0]
    d = lax.axis_index("dev")
    first_nnz = d * nnz_here
    band_rows = pointer.shape[1] - 1

    def count(limit):
        def add(r, total):
            return total + jnp.where(pointer[0, r + 1] <= limit, 1, 0)

        return lax.fori_loop(0, band_rows, add, jnp.int32(0))

    first = count(first_nnz)
    finished = count(first_nnz + nnz_here) - first
    past = pltpu.make_async_copy(before.at[pl.ds(band_rows + first, SPAN)], older, sems.at[CHUNKS + 1])
    past.start()
    base, ready = fetch(sizes, blocks, window, held, near, sems)
    past.wait()

    def one(row):
        begin, end = bounds(pointer, row, first_nnz, nnz_here)
        ready(begin, end)
        return row_sum(begin, end, row + band_rows - base, offsets, held, near)

    @pl.loop(0, SPAN)
    def _(slot):
        filled = slot < finished
        row = first + slot

        @pl.when(filled)
        def _():
            present = near[row + band_rows - base].astype(jnp.float32)
            value = 2.0 * (one(row) - CENTER * present) / HALFWIDTH - older[slot].astype(jnp.float32)
            filtered[slot] = value.astype(filtered.dtype)

            @pl.when(slot == 0)
            def _():
                head[0] = value

        @pl.when(jnp.logical_not(filled))
        def _():
            filtered[slot] = jnp.zeros(filtered.shape[1:], filtered.dtype)

    tail[0] = one(first + finished).astype(tail.dtype)


def local(n_grp, n_dev, row_ptr, col_off, blocks, trial):
    nnz_here, blk, _ = blocks.shape
    vectors = trial.shape[1]
    band_rows = row_ptr.shape[1] - 1
    rb = band_rows // n_dev
    half = max(FLOOR, band_rows // 2)
    reach = -(-half // rb)
    low, high = 1 + reach, 2 + reach
    _, y_count = grid_of(n_dev)
    own_rows = trial.reshape(rb, blk, vectors)
    sizes = (rb, n_grp, n_dev, low, high)
    near_rows = (low + high) * rb + 1
    dma = pltpu.SemaphoreType.DMA
    sems = [
        dma((n_dev, rb)), dma((2, n_dev)), dma((2, n_dev)), dma((max(1, y_count - 1), n_dev)), dma((2, n_dev)), dma,
    ]
    any_spec = pl.BlockSpec(memory_space=pl.ANY)
    vmem = pl.BlockSpec(memory_space=pltpu.VMEM)
    smem = pl.BlockSpec(memory_space=pltpu.SMEM)
    kept = trial.dtype

    def shape(rows, dtype):
        return jax.ShapeDtypeStruct((rows, blk, vectors), dtype)

    def buffer(rows, dtype):
        return pltpu.VMEM((rows, blk, vectors), dtype)

    def remote(collective_id):
        return pltpu.CompilerParams(
            collective_id=collective_id, has_side_effects=True, vmem_limit_bytes=VMEM_BYTES
        )

    here = pltpu.CompilerParams(vmem_limit_bytes=VMEM_BYTES)
    first = pl.pallas_call(
        functools.partial(first_kernel, sizes),
        out_shape=shape(3 * band_rows, kept),
        in_specs=[any_spec],
        out_specs=any_spec,
        scratch_shapes=sems,
        compiler_params=remote(0),
        name="spread_trial",
    )(own_rows)
    left, own, right = pl.pallas_call(
        functools.partial(frame_kernel, sizes),
        out_shape=(shape(rb, kept), shape(rb, jnp.float32), shape(rb + 1, kept)),
        in_specs=[smem] * 2 + [any_spec] * 2,
        out_specs=(vmem, vmem, vmem),
        scratch_shapes=[pltpu.VMEM(blocks.shape, blocks.dtype), buffer(near_rows, kept), dma((CHUNKS + 1,))],
        compiler_params=here,
        name="sums_first",
    )(row_ptr, col_off, blocks, first)
    second = pl.pallas_call(
        functools.partial(second_kernel, sizes),
        out_shape=shape(3 * band_rows, kept),
        in_specs=[vmem] * 4,
        out_specs=any_spec,
        scratch_shapes=[buffer(rb, kept)] * 3 + [buffer(1, kept), dma((3, rb)), dma((3, rb)), buffer(rb, jnp.float32)] + sems,
        compiler_params=remote(1),
        name="finish_and_spread",
    )(left, own, right, own_rows)
    filtered, head, tail = pl.pallas_call(
        functools.partial(slots_kernel, sizes),
        out_shape=(shape(SPAN, kept), shape(1, jnp.float32), shape(1, kept)),
        in_specs=[smem] * 2 + [any_spec] * 3,
        out_specs=(vmem, vmem, vmem),
        scratch_shapes=[
            pltpu.VMEM(blocks.shape, blocks.dtype), buffer(near_rows, kept), buffer(SPAN, kept), dma((CHUNKS + 2,)),
        ],
        compiler_params=here,
        name="sums_second",
    )(row_ptr, col_off, blocks, second, first)
    carried = lax.ppermute(tail, "dev", [(i, i + 1) for i in range(n_dev - 1)])
    start = (head + carried.astype(jnp.float32) * (2.0 / HALFWIDTH)).astype(kept)
    filtered = lax.dynamic_update_slice_in_dim(filtered, start, 0, 0)
    return filtered.reshape(SPAN * blk, vectors)


def solution(mesh):
    in_specs = (
        P("grp", None),
        P("grp", "dev"),
        P(("grp", "dev"), None, None),
        P(("grp", "dev"), None),
    )
    step = functools.partial(local, mesh.shape["grp"], mesh.shape["dev"])
    return jax.shard_map(step, mesh=mesh, in_specs=in_specs, out_specs=P(("grp", "dev"), None), check_vma=False)
```

time: 127 us -> 98.5 us (0.78)
  Pallas kernels: 105 us -> 88.4 us
  local copies, waits for them, and re-layouts: 6.43 us -> 0 us
  other arithmetic: 7.83 us -> 1.55 us
    pallas_call x3, Pallas kernels: 70.7 us -> 57.7 us  [the longest x1 41.9 us: local(): pl.pallas_call(functools.partial(second_kernel, sizes), out_shape=shape(3...]
    gather x4 -> x0, local copies, waits for them, and re-layouts: 3.93 us -> none  [the longest x2 2.62 us: segments(): begin = jnp.clip(pointer[safe] - first_nnz, 0, nnz_here)]
    pallas_call x1, Pallas kernels: 34.4 us -> 30.8 us  [local(): pl.pallas_call(functools.partial(first_kernel, sizes), out_shape=shape(3...]
    convert_element_type x1 -> x0, other arithmetic: 2.02 us -> none  [local(): return result.astype(kept).reshape(SPAN * blk, vectors)]
    select_n x5 -> x0, other arithmetic: 1.87 us -> none  [the longest x1 1.23 us: local(): jnp.where((slot_ids < finished) | (slot_ids == SPAN), slot_ends, slot_sta...]
    dynamic_slice x1 -> x0, local copies, waits for them, and re-layouts: 1.77 us -> none  [local(): older = lax.dynamic_slice_in_dim(window, places[0], SPAN, 0)]
    dynamic_update_slice x0 -> x1, other arithmetic: none -> 1.55 us  [local(): filtered = lax.dynamic_update_slice_in_dim(filtered, start, 0, 0)]
    reduce_sum x2 -> x0, other arithmetic: 1.45 us -> none  [the longest x1 1.36 us: local(): jnp.sum(((row_ends > first_nnz) & (row_ends <= first_nnz + nnz_here)).ast...]
where the time goes in v2:
time: 98.5 us; the launch traced here: 96.7 us
  Pallas kernels  88.4 us (90%)
  waiting for transfers between devices  4.11 us (4%)
  starting transfers between devices  2.54 us (3%)
  other arithmetic  1.55 us (2%)
    pallas_call x1, Pallas kernels, local(): pl.pallas_call(functools.partial(second_kernel, sizes), out_shape=shape(3...  41.9 us
    pallas_call x1, Pallas kernels, local(): pl.pallas_call(functools.partial(first_kernel, sizes), out_shape=shape(3...  30.8 us
    pallas_call x1, Pallas kernels, local(): pl.pallas_call(functools.partial(slots_kernel, sizes), out_shape=(shape(S...  8.1 us
    pallas_call x1, Pallas kernels, local(): pl.pallas_call(functools.partial(frame_kernel, sizes), out_shape=(shape(r...  7.66 us
    ppermute x1, waiting for transfers between devices, local(): carried = lax.ppermute(tail, 'dev', [(i, i + 1) for i in range(n_dev - 1)])  4.11 us
    ppermute x1, starting transfers between devices, local(): carried = lax.ppermute(tail, 'dev', [(i, i + 1) for i in range(n_dev - 1)])  2.54 us
  transfers between devices with their start and end apart: 1, of which 1 were waited for; matrix products, arithmetic and copies ran while one was open for 0% of the time, Pallas kernels for 0%

profile of v2, /device:TPU:27, one launch (start us, length us, event | category | flops | bytes accessed | tf_op | source)
XLA Modules:
  0.0 96.7 jit_solution(17923727053688949145)
XLA Ops:
  0.0 30.8 %spread_trial.1.window.before = bf16[96,128,256]{2,1,0:T(8,128)(2,1)} custom-call(bf16[4,128,256]{2,1,0:T(8,128)(2,1)} %bitcast.2), custom_call_target="tpu_custom_call" | custom-call | tf_op jit(solution)/shard_map/spread_trial/pallas_call | solution.py:370
  30.8 7.7 %sums_first.1 = (bf16[4,128,256]{2,1,0:T(8,128)(2,1)}, f32[4,128,256]{2,1,0:T(8,128)}, bf16[5,128,256]{2,1,0:T(8,128)(2,1)}) custom-call(s32[1,33]{1,0:T(1,128)} %pointer.3, s32[1,128]{1,0:T(1,128)} %offsets.3, bf16[128,128,128]{2,1,0:T(8,128)(2,1)} %blocks.3, bf16[96,128,256]{2,1,0:T(8,128)(2,1)} %spread_trial.1.window.before), custom_call_target="tpu_custom_call" | custom-call | tf_op jit(solution)/shard_map/sums_first/pallas_call | solution.py:379
  38.4 41.9 %finish_and_spread.1.window = bf16[96,128,256]{2,1,0:T(8,128)(2,1)} custom-call(bf16[4,128,256]{2,1,0:T(8,128)(2,1)} %get-tuple-element.11.left, f32[4,128,256]{2,1,0:T(8,128)} %get-tuple-element.12.own, bf16[5,128,256]{2,1,0:T(8,128)(2,1)} %get-tuple-element.13.right, bf16[4,128,256]{2,1,0:T(8,128)(2,1)} %bitcast.3), custom_call_target="tpu_custom_call" | custom-call | tf_op jit(solution)/shard_map/finish_and_spread/pallas_call | solution.py:388
  80.4 8.1 %sums_second.1 = (bf16[6,128,256]{2,1,0:T(8,128)(2,1)}, f32[1,128,256]{2,1,0:T(8,128)}, bf16[1,128,256]{2,1,0:T(8,128)(2,1)}) custom-call(s32[1,33]{1,0:T(1,128)} %pointer.3, s32[1,128]{1,0:T(1,128)} %offsets.3, bf16[128,128,128]{2,1,0:T(8,128)(2,1)} %blocks.3, bf16[96,128,256]{2,1,0:T(8,128)(2,1)} %finish_and_spread.1.window, ...), custom_call_target="tpu_custom_call" | custom-call | tf_op jit(solution)/shard_map/sums_second/pallas_call | solution.py:397
  88.5 2.5 %collective-permute-start = (bf16[1,128,256]{2,1,0:T(8,128)(2,1)}, bf16[1,128,256]{2,1,0:T(8,128)(2,1)S(1)}, u32[]{:S(2)}, u32[]{:S(2)}) collective-permute-start(bf16[1,128,256]{2,1,0:T(8,128)(2,1)} %get-tuple-element.16), channel_id=1, source_target_pairs={{0,1},{1,2},{2,3},{3,4},{4,5},{5,6},{6,7},{8,9},{9,10},{10,11},{11... | collective-permute-start | bytes 196616 | tf_op jit(solution)/shard_map/ppermute | solution.py:408
  91.0 4.1 %collective-permute-done = bf16[1,128,256]{2,1,0:T(8,128)(2,1)S(1)} collective-permute-done((bf16[1,128,256]{2,1,0:T(8,128)(2,1)}, bf16[1,128,256]{2,1,0:T(8,128)(2,1)S(1)}, u32[]{:S(2)}, u32[]{:S(2)}) %collective-permute-start) | collective-permute-done | bytes 65568 | tf_op jit(solution)/shard_map/ppermute | solution.py:408
  95.1 1.6 %fusion = bf16[6,128,256]{2,1,0:T(8,128)(2,1)} fusion(bf16[6,128,256]{2,1,0:T(8,128)(2,1)} %get-tuple-element.14, f32[1,128,256]{2,1,0:T(8,128)} %get-tuple-element.15, bf16[1,128,256]{2,1,0:T(8,128)(2,1)S(1)} %collective-permute-done), kind=kLoop, calls=%fused_computation.1 | loop fusion | flops 131072 | bytes 262144 | tf_op jit(solution)/shard_map/dynamic_update_slice | solution.py:410
Async XLA Ops:
  88.5 6.7 %collective-permute-start = (bf16[1,128,256]{2,1,0:T(8,128)(2,1)}, bf16[1,128,256]{2,1,0:T(8,128)(2,1)S(1)}, u32[]{:S(2)}, u32[]{:S(2)}) collective-permute-start(bf16[1,128,256]{2,1,0:T(8,128)(2,1)} %get-tuple-element.16), channel_id=1, source_target_pairs={{0,1},{1,2},{2,3},{3,4},{4,5},{5,6},{6,7},{8,9},{9,10},{10,11},{11... | collective-permute-start | bytes 196616 | tf_op jit(solution)/shard_map/ppermute | solution.py:408

commit v3 on v2

--- a/solution.py
+++ b/solution.py
@@ -11,6 +11,7 @@
 CENTER = 0.5
 HALFWIDTH = 1.5
 FLOOR = 24
+ROW_MAX = 48
 DEPTH = 16
 CHUNKS = 4
 VMEM_BYTES = 56 * 1024 * 1024
@@ -31,7 +32,7 @@
     z, y = d // y_count, lax.rem(d, y_count)
     after = lax.rem(g + 1, n_grp)
     before = lax.rem(g + n_grp - 1, n_grp)
-    sends = []
+    early = max(1, rb // 4) if y_count > 1 else 0
 
     def rows(slot, p=None, count=1):
         return window.at[pl.ds(slot * rb, rb)] if p is None else window.at[pl.ds(slot * rb + p, count)]
@@ -55,15 +56,21 @@
             send_side.at[1, s], recv_side.at[1, s], (before, d),
         )
 
-    def line_step(cond, s, p, way, src):
+    def along(cond, s, p, way, src):
         dst = rows(n_dev + s, p)
         if way >= 0:
             post(cond & (z < z_count - 1), src, dst, send_z.at[0, s], recv_own.at[s, p], (g, d + y_count))
         if way <= 0:
             post(cond & (z > 0), src, dst, send_z.at[1, s], recv_own.at[s, p], (g, d - y_count))
+
+    def line_step(cond, s, p, way, src):
+        along(cond, s, p, way, src)
         for step in range(1, y_count):
             other = z * y_count + lax.rem(y + step, y_count)
-            post(cond, src, dst, send_y.at[step - 1, s], recv_own.at[s, p], (g, other))
+            post(
+                cond if way == 0 else cond & (p >= early), src, rows(n_dev + s, p),
+                send_y.at[step - 1, s], recv_own.at[s, p], (g, other),
+            )
         to_sides(cond, s, p, src)
 
     def around(k):
@@ -72,11 +79,12 @@
         return [(z - k >= 0, z - k, 1), (z + k < z_count, z + k, -1)]
 
     def across(k, p):
-        for cond, at, _ in around(k):
+        for cond, at, way in around(k):
             at = jnp.clip(at, 0, z_count - 1)
             for step in range(1, y_count):
                 s = at * y_count + lax.rem(y + step, y_count)
                 drain(cond, rows(n_dev + s, p), recv_own.at[s, p])
+                along(cond & (p < early), s, p, way, rows(n_dev + s, p))
                 to_sides(cond, s, p, rows(n_dev + s, p))
 
     @pl.loop(0, rb)
@@ -110,11 +118,15 @@
         drain(low_in, shard, send_side.at[0, s])
         drain(high_in, later, send_side.at[1, s])
         drain(edge_in, one, send_side.at[1, s])
-        mine_line = s_y == y
-        drain(mine_line & (s_z <= z) & (z < z_count - 1), shard, send_z.at[0, s])
-        drain(mine_line & (s_z >= z) & (z > 0), shard, send_z.at[1, s])
+        first, rest = window.at[pl.ds(s * rb, max(1, early))], window.at[pl.ds(s * rb, rb - early)]
+        line = s_y == y
+        for way, cond in ((0, (s_z <= z) & (z < z_count - 1)), (1, (s_z >= z) & (z > 0))):
+            drain(cond & line, shard, send_z.at[way, s])
+            if early:
+                drain(cond & jnp.logical_not(line), first, send_z.at[way, s])
         for step in range(1, y_count):
-            drain(mine_line, shard, send_y.at[step - 1, s])
+            drain(s == d, shard, send_y.at[step - 1, s])
+            drain(line & (s != d), rest, send_y.at[step - 1, s])
 
     keep.wait()
 
@@ -244,14 +256,14 @@
     return begin, jnp.where((row >= 0) & (row < count), end, begin)
 
 
-def row_sum(begin, end, shift, offsets, held, near):
+def row_sum(begin, end, shift, offsets, held, near, skipped=0):
     def step(i, total):
         lhs, rhs = [], []
         for j in range(DEPTH):
             b = begin + i * DEPTH + j
             valid = b < end
             b = jnp.minimum(b, end - 1)
-            block = held[b]
+            block = held[b - skipped]
             lhs.append(jnp.where(valid, block, jnp.zeros_like(block)))
             rhs.append(near[offsets[0, b] + shift])
         return total + jnp.dot(
@@ -287,21 +299,41 @@
         right[at] = one(2 * rb + at).astype(right.dtype)
 
 
-def slots_kernel(sizes, pointer, offsets, blocks, window, before, filtered, head, tail, held, near, older, sems):
+def rows_ended(pointer, limit):
+    def add(r, total):
+        return total + jnp.where(pointer[0, r + 1] <= limit, 1, 0)
+
+    return lax.fori_loop(0, pointer.shape[1] - 1, add, jnp.int32(0))
+
+
+def tail_kernel(sizes, pointer, offsets, blocks, window, tail, held, near, sems):
+    rb, n_grp, n_dev, low, high = sizes
+    nnz_here = blocks.shape[0]
+    skipped = nnz_here - held.shape[0]
+    d = lax.axis_index("dev")
+    row = rows_ended(pointer, (d + 1) * nnz_here)
+    reach = high - 2
+    base = (n_dev - reach) * rb + row
+    base = jnp.minimum(base, (n_dev + d + high) * rb + 1 - near.shape[0])
+    some = pltpu.make_async_copy(blocks.at[pl.ds(skipped, held.shape[0])], held, sems.at[0])
+    some.start()
+    rows = pltpu.make_async_copy(window.at[pl.ds(base, near.shape[0])], near, sems.at[1])
+    rows.start()
+    begin, end = bounds(pointer, row, d * nnz_here, nnz_here)
+    some.wait()
+    rows.wait()
+    tail[0] = row_sum(begin, end, row + n_dev * rb - base, offsets, held, near, skipped).astype(tail.dtype)
+
+
+def slots_kernel(sizes, pointer, offsets, blocks, window, before, filtered, head, held, near, older, sems):
     rb, n_grp, n_dev, low, high = sizes
     nnz_here = blocks.shape[0]
     d = lax.axis_index("dev")
     first_nnz = d * nnz_here
     band_rows = pointer.shape[1] - 1
 
-    def count(limit):
-        def add(r, total):
-            return total + jnp.where(pointer[0, r + 1] <= limit, 1, 0)
-
-        return lax.fori_loop(0, band_rows, add, jnp.int32(0))
-
-    first = count(first_nnz)
-    finished = count(first_nnz + nnz_here) - first
+    first = rows_ended(pointer, first_nnz)
+    finished = rows_ended(pointer, first_nnz + nnz_here) - first
     past = pltpu.make_async_copy(before.at[pl.ds(band_rows + first, SPAN)], older, sems.at[CHUNKS + 1])
     past.start()
     base, ready = fetch(sizes, blocks, window, held, near, sems)
@@ -331,7 +363,7 @@
         def _():
             filtered[slot] = jnp.zeros(filtered.shape[1:], filtered.dtype)
 
-    tail[0] = one(first + finished).astype(tail.dtype)
+    ready(*bounds(pointer, first + finished, first_nnz, nnz_here))
 
 
 def local(n_grp, n_dev, row_ptr, col_off, blocks, trial):
@@ -394,18 +426,36 @@
         compiler_params=remote(1),
         name="finish_and_spread",
     )(left, own, right, own_rows)
-    filtered, head, tail = pl.pallas_call(
+    tail_blocks = min(ROW_MAX, nnz_here)
+    tail = pl.pallas_call(
+        functools.partial(tail_kernel, sizes),
+        out_shape=shape(1, kept),
+        in_specs=[smem] * 2 + [any_spec] * 2,
+        out_specs=vmem,
+        scratch_shapes=[pltpu.VMEM((tail_blocks,) + blocks.shape[1:], blocks.dtype), buffer(2 * reach * rb + 1, kept), dma((2,))],
+        compiler_params=here,
+        cost_estimate=pl.CostEstimate(
+            flops=2 * tail_blocks * blk * blk * vectors, bytes_accessed=2 * blk * (tail_blocks * blk + (2 * reach * rb + 1) * vectors),
+            transcendentals=0,
+        ),
+        name="tail_sum",
+    )(row_ptr, col_off, blocks, second)
+    carried = lax.ppermute(tail, "dev", [(i, i + 1) for i in range(n_dev - 1)])
+    filtered, head = pl.pallas_call(
         functools.partial(slots_kernel, sizes),
-        out_shape=(shape(SPAN, kept), shape(1, jnp.float32), shape(1, kept)),
+        out_shape=(shape(SPAN, kept), shape(1, jnp.float32)),
         in_specs=[smem] * 2 + [any_spec] * 3,
-        out_specs=(vmem, vmem, vmem),
+        out_specs=(vmem, vmem),
         scratch_shapes=[
             pltpu.VMEM(blocks.shape, blocks.dtype), buffer(near_rows, kept), buffer(SPAN, kept), dma((CHUNKS + 2,)),
         ],
         compiler_params=here,
+        cost_estimate=pl.CostEstimate(
+            flops=8 * nnz_here * blk * blk * vectors, bytes_accessed=2 * blk * (nnz_here * blk + near_rows * vectors),
+            transcendentals=0,
+        ),
         name="sums_second",
     )(row_ptr, col_off, blocks, second, first)
-    carried = lax.ppermute(tail, "dev", [(i, i + 1) for i in range(n_dev - 1)])
     start = (head + carried.astype(jnp.float32) * (2.0 / HALFWIDTH)).astype(kept)
     filtered = lax.dynamic_update_slice_in_dim(filtered, start, 0, 0)
     return filtered.reshape(SPAN * blk, vectors)

time: 98.5 us -> 98.9 us (level)
  Pallas kernels: 88.4 us -> 93.4 us
  waiting for transfers between devices: 4.11 us -> 0.01 us
    pallas_call x0 -> x1, Pallas kernels: none -> 4.28 us  [local(): pl.pallas_call(functools.partial(tail_kernel, sizes), out_shape=shape(1,...]
    ppermute x1, waiting for transfers between devices: 4.11 us -> 0.01 us  [local(): carried = lax.ppermute(tail, 'dev', [(i, i + 1) for i in range(n_dev - 1)])]
    pallas_call x1, Pallas kernels: 41.9 us -> 40.9 us  [local(): pl.pallas_call(functools.partial(second_kernel, sizes), out_shape=shape(3...]
  transfers between devices with their start and end apart: 1 -> 1, of which waited for: 1 -> 0; matrix products, arithmetic and copies ran while one was open for 0% -> 0% of each run, Pallas kernels for 0% -> 9%
where the time goes in v3:
time: 98.9 us; the launch traced here: 97.3 us
  Pallas kernels  93.4 us (94%)
  starting transfers between devices  2.35 us (2%)
  other arithmetic  1.56 us (2%)
    pallas_call x1, Pallas kernels, local(): pl.pallas_call(functools.partial(second_kernel, sizes), out_shape=shape(3...  40.9 us
    pallas_call x1, Pallas kernels, local(): pl.pallas_call(functools.partial(first_kernel, sizes), out_shape=shape(3...  31.6 us
    pallas_call x1, Pallas kernels, local(): pl.pallas_call(functools.partial(slots_kernel, sizes), out_shape=(shape(S...  8.38 us
    pallas_call x1, Pallas kernels, local(): pl.pallas_call(functools.partial(frame_kernel, sizes), out_shape=(shape(r...  8.28 us
    pallas_call x1, Pallas kernels, local(): pl.pallas_call(functools.partial(tail_kernel, sizes), out_shape=shape(1,...  4.28 us
    ppermute x1, starting transfers between devices, local(): carried = lax.ppermute(tail, 'dev', [(i, i + 1) for i in range(n_dev - 1)])  2.35 us
  transfers between devices with their start and end apart: 1, of which 0 were waited for; matrix products, arithmetic and copies ran while one was open for 0% of the time, Pallas kernels for 9%

profile of v3, /device:TPU:27, one launch (start us, length us, event | category | flops | bytes accessed | tf_op | source)
XLA Modules:
  0.0 97.3 jit_solution(12040581396879267808)
XLA Ops:
  0.0 31.6 %spread_trial.1.window.before = bf16[96,128,256]{2,1,0:T(8,128)(2,1)} custom-call(bf16[4,128,256]{2,1,0:T(8,128)(2,1)} %bitcast.2), custom_call_target="tpu_custom_call" | custom-call | tf_op jit(solution)/shard_map/spread_trial/pallas_call | solution.py:402
  31.6 8.3 %sums_first.1 = (bf16[4,128,256]{2,1,0:T(8,128)(2,1)}, f32[4,128,256]{2,1,0:T(8,128)}, bf16[5,128,256]{2,1,0:T(8,128)(2,1)}) custom-call(s32[1,33]{1,0:T(1,128)} %pointer.5, s32[1,128]{1,0:T(1,128)} %offsets.5, bf16[128,128,128]{2,1,0:T(8,128)(2,1)} %blocks.5, bf16[96,128,256]{2,1,0:T(8,128)(2,1)} %spread_trial.1.window.before), custom_call_target="tpu_custom_call" | custom-call | tf_op jit(solution)/shard_map/sums_first/pallas_call | solution.py:411
  39.9 40.9 %finish_and_spread.1.window = bf16[96,128,256]{2,1,0:T(8,128)(2,1)} custom-call(bf16[4,128,256]{2,1,0:T(8,128)(2,1)} %get-tuple-element.10.left, f32[4,128,256]{2,1,0:T(8,128)} %get-tuple-element.11.own, bf16[5,128,256]{2,1,0:T(8,128)(2,1)} %get-tuple-element.12.right, bf16[4,128,256]{2,1,0:T(8,128)(2,1)} %bitcast.3), custom_call_target="tpu_custom_call" | custom-call | tf_op jit(solution)/shard_map/finish_and_spread/pallas_call | solution.py:420
  80.7 4.3 %tail_sum.1 = bf16[1,128,256]{2,1,0:T(8,128)(2,1)} custom-call(s32[1,33]{1,0:T(1,128)} %pointer.5, s32[1,128]{1,0:T(1,128)} %offsets.5, bf16[128,128,128]{2,1,0:T(8,128)(2,1)} %blocks.5, bf16[96,128,256]{2,1,0:T(8,128)(2,1)} %finish_and_spread.1.window), custom_call_target="tpu_custom_call" | custom-call | flops 402653184 | bytes 4784128 | tf_op jit(solution)/shard_map/tail_sum/pallas_call | solution.py:430
  85.0 2.4 %collective-permute-start = (bf16[1,128,256]{2,1,0:T(8,128)(2,1)}, bf16[1,128,256]{2,1,0:T(8,128)(2,1)S(1)}, u32[]{:S(2)}, u32[]{:S(2)}) collective-permute-start(bf16[1,128,256]{2,1,0:T(8,128)(2,1)} %tail_sum.1), channel_id=1, source_target_pairs={{0,1},{1,2},{2,3},{3,4},{4,5},{5,6},{6,7},{8,9},{9,10},{10,11},{11... | collective-permute-start | bytes 196616 | tf_op jit(solution)/shard_map/ppermute | solution.py:443
  87.4 8.4 %sums_second.1 = (bf16[6,128,256]{2,1,0:T(8,128)(2,1)}, f32[1,128,256]{2,1,0:T(8,128)}) custom-call(s32[1,33]{1,0:T(1,128)} %pointer.5, s32[1,128]{1,0:T(1,128)} %offsets.5, bf16[128,128,128]{2,1,0:T(8,128)(2,1)} %blocks.5, bf16[96,128,256]{2,1,0:T(8,128)(2,1)} %finish_and_spread.1.window, bf16[96,128,256]{2,1,0:T(8,128)(2,1)} %spread_trial.1.window.before), custom_call_target="tpu_custom_call" | custom-call | flops 4294967296 | bytes 8192000 | tf_op jit(solution)/shard_map/sums_second/pallas_call | solution.py:444
  95.8 0.0 collective-permute-done
  95.8 1.6 %fusion = bf16[6,128,256]{2,1,0:T(8,128)(2,1)} fusion(bf16[6,128,256]{2,1,0:T(8,128)(2,1)} %get-tuple-element.13, f32[1,128,256]{2,1,0:T(8,128)} %get-tuple-element.14, bf16[1,128,256]{2,1,0:T(8,128)(2,1)S(1)} %collective-permute-done), kind=kLoop, calls=%fused_computation.1 | loop fusion | flops 131072 | bytes 262144 | tf_op jit(solution)/shard_map/dynamic_update_slice | solution.py:460
Async XLA Ops:
  85.0 10.8 %collective-permute-start = (bf16[1,128,256]{2,1,0:T(8,128)(2,1)}, bf16[1,128,256]{2,1,0:T(8,128)(2,1)S(1)}, u32[]{:S(2)}, u32[]{:S(2)}) collective-permute-start(bf16[1,128,256]{2,1,0:T(8,128)(2,1)} %tail_sum.1), channel_id=1, source_target_pairs={{0,1},{1,2},{2,3},{3,4},{4,5},{5,6},{6,7},{8,9},{9,10},{10,11},{11... | collective-permute-start | bytes 196616 | tf_op jit(solution)/shard_map/ppermute | solution.py:443

commit v4 on v2

--- a/solution.py
+++ b/solution.py
@@ -31,7 +31,7 @@
     z, y = d // y_count, lax.rem(d, y_count)
     after = lax.rem(g + 1, n_grp)
     before = lax.rem(g + n_grp - 1, n_grp)
-    sends = []
+    early = rb // 4 if y_count > 1 and prepare is not None else 0
 
     def rows(slot, p=None, count=1):
         return window.at[pl.ds(slot * rb, rb)] if p is None else window.at[pl.ds(slot * rb + p, count)]
@@ -55,15 +55,21 @@
             send_side.at[1, s], recv_side.at[1, s], (before, d),
         )
 
-    def line_step(cond, s, p, way, src):
+    def along(cond, s, p, way, src):
         dst = rows(n_dev + s, p)
         if way >= 0:
             post(cond & (z < z_count - 1), src, dst, send_z.at[0, s], recv_own.at[s, p], (g, d + y_count))
         if way <= 0:
             post(cond & (z > 0), src, dst, send_z.at[1, s], recv_own.at[s, p], (g, d - y_count))
+
+    def line_step(cond, s, p, way, src):
+        along(cond, s, p, way, src)
         for step in range(1, y_count):
             other = z * y_count + lax.rem(y + step, y_count)
-            post(cond, src, dst, send_y.at[step - 1, s], recv_own.at[s, p], (g, other))
+            post(
+                cond if way == 0 else cond & (p >= early), src, rows(n_dev + s, p),
+                send_y.at[step - 1, s], recv_own.at[s, p], (g, other),
+            )
         to_sides(cond, s, p, src)
 
     def around(k):
@@ -72,11 +78,12 @@
         return [(z - k >= 0, z - k, 1), (z + k < z_count, z + k, -1)]
 
     def across(k, p):
-        for cond, at, _ in around(k):
+        for cond, at, way in around(k):
             at = jnp.clip(at, 0, z_count - 1)
             for step in range(1, y_count):
                 s = at * y_count + lax.rem(y + step, y_count)
                 drain(cond, rows(n_dev + s, p), recv_own.at[s, p])
+                along(cond & (p < early), s, p, way, rows(n_dev + s, p))
                 to_sides(cond, s, p, rows(n_dev + s, p))
 
     @pl.loop(0, rb)
@@ -110,11 +117,15 @@
         drain(low_in, shard, send_side.at[0, s])
         drain(high_in, later, send_side.at[1, s])
         drain(edge_in, one, send_side.at[1, s])
-        mine_line = s_y == y
-        drain(mine_line & (s_z <= z) & (z < z_count - 1), shard, send_z.at[0, s])
-        drain(mine_line & (s_z >= z) & (z > 0), shard, send_z.at[1, s])
+        first, rest = window.at[pl.ds(s * rb, max(1, early))], window.at[pl.ds(s * rb, rb - early)]
+        line = s_y == y
+        for way, cond in ((0, (s_z <= z) & (z < z_count - 1)), (1, (s_z >= z) & (z > 0))):
+            drain(cond & line, shard, send_z.at[way, s])
+            if early:
+                drain(cond & jnp.logical_not(line), first, send_z.at[way, s])
         for step in range(1, y_count):
-            drain(mine_line, shard, send_y.at[step - 1, s])
+            drain(s == d, shard, send_y.at[step - 1, s])
+            drain(line & (s != d), rest, send_y.at[step - 1, s])
 
     keep.wait()
 

time: 98.5 us -> 97.5 us (0.990); the launches traced: 96.7 us -> 96.9 us
  no operation moved by 1% of the time
where the time goes in v4:
time: 97.5 us; the launch traced here: 96.9 us
  Pallas kernels  89.2 us (91%)
  waiting for transfers between devices  4.06 us (4%)
  starting transfers between devices  2.06 us (2%)
  other arithmetic  1.55 us (2%)
    pallas_call x1, Pallas kernels, local(): pl.pallas_call(functools.partial(second_kernel, sizes), out_shape=shape(3...  41.4 us
    pallas_call x1, Pallas kernels, local(): pl.pallas_call(functools.partial(first_kernel, sizes), out_shape=shape(3...  30.8 us
    pallas_call x1, Pallas kernels, local(): pl.pallas_call(functools.partial(slots_kernel, sizes), out_shape=(shape(S...  8.73 us
    pallas_call x1, Pallas kernels, local(): pl.pallas_call(functools.partial(frame_kernel, sizes), out_shape=(shape(r...  8.28 us
    ppermute x1, waiting for transfers between devices, local(): carried = lax.ppermute(tail, 'dev', [(i, i + 1) for i in range(n_dev - 1)])  4.06 us
    ppermute x1, starting transfers between devices, local(): carried = lax.ppermute(tail, 'dev', [(i, i + 1) for i in range(n_dev - 1)])  2.06 us
  transfers between devices with their start and end apart: 1, of which 1 were waited for; matrix products, arithmetic and copies ran while one was open for 0% of the time, Pallas kernels for 0%

profile of v4, /device:TPU:27, one launch (start us, length us, event | category | flops | bytes accessed | tf_op | source)
XLA Modules:
  0.0 96.9 jit_solution(6721430560730691309)
XLA Ops:
  0.0 30.8 %spread_trial.1.window.before = bf16[96,128,256]{2,1,0:T(8,128)(2,1)} custom-call(bf16[4,128,256]{2,1,0:T(8,128)(2,1)} %bitcast.2), custom_call_target="tpu_custom_call" | custom-call | tf_op jit(solution)/shard_map/spread_trial/pallas_call | solution.py:381
  30.8 8.3 %sums_first.1 = (bf16[4,128,256]{2,1,0:T(8,128)(2,1)}, f32[4,128,256]{2,1,0:T(8,128)}, bf16[5,128,256]{2,1,0:T(8,128)(2,1)}) custom-call(s32[1,33]{1,0:T(1,128)} %pointer.3, s32[1,128]{1,0:T(1,128)} %offsets.3, bf16[128,128,128]{2,1,0:T(8,128)(2,1)} %blocks.3, bf16[96,128,256]{2,1,0:T(8,128)(2,1)} %spread_trial.1.window.before), custom_call_target="tpu_custom_call" | custom-call | tf_op jit(solution)/shard_map/sums_first/pallas_call | solution.py:390
  39.1 41.4 %finish_and_spread.1.window = bf16[96,128,256]{2,1,0:T(8,128)(2,1)} custom-call(bf16[4,128,256]{2,1,0:T(8,128)(2,1)} %get-tuple-element.11.left, f32[4,128,256]{2,1,0:T(8,128)} %get-tuple-element.12.own, bf16[5,128,256]{2,1,0:T(8,128)(2,1)} %get-tuple-element.13.right, bf16[4,128,256]{2,1,0:T(8,128)(2,1)} %bitcast.3), custom_call_target="tpu_custom_call" | custom-call | tf_op jit(solution)/shard_map/finish_and_spread/pallas_call | solution.py:399
  80.5 8.7 %sums_second.1 = (bf16[6,128,256]{2,1,0:T(8,128)(2,1)}, f32[1,128,256]{2,1,0:T(8,128)}, bf16[1,128,256]{2,1,0:T(8,128)(2,1)}) custom-call(s32[1,33]{1,0:T(1,128)} %pointer.3, s32[1,128]{1,0:T(1,128)} %offsets.3, bf16[128,128,128]{2,1,0:T(8,128)(2,1)} %blocks.3, bf16[96,128,256]{2,1,0:T(8,128)(2,1)} %finish_and_spread.1.window, ...), custom_call_target="tpu_custom_call" | custom-call | tf_op jit(solution)/shard_map/sums_second/pallas_call | solution.py:408
  89.2 2.1 %collective-permute-start = (bf16[1,128,256]{2,1,0:T(8,128)(2,1)}, bf16[1,128,256]{2,1,0:T(8,128)(2,1)S(1)}, u32[]{:S(2)}, u32[]{:S(2)}) collective-permute-start(bf16[1,128,256]{2,1,0:T(8,128)(2,1)} %get-tuple-element.16), channel_id=1, source_target_pairs={{0,1},{1,2},{2,3},{3,4},{4,5},{5,6},{6,7},{8,9},{9,10},{10,11},{11... | collective-permute-start | bytes 196616 | tf_op jit(solution)/shard_map/ppermute | solution.py:419
  91.3 4.1 %collective-permute-done = bf16[1,128,256]{2,1,0:T(8,128)(2,1)S(1)} collective-permute-done((bf16[1,128,256]{2,1,0:T(8,128)(2,1)}, bf16[1,128,256]{2,1,0:T(8,128)(2,1)S(1)}, u32[]{:S(2)}, u32[]{:S(2)}) %collective-permute-start) | collective-permute-done | bytes 65568 | tf_op jit(solution)/shard_map/ppermute | solution.py:419
  95.3 1.6 %fusion = bf16[6,128,256]{2,1,0:T(8,128)(2,1)} fusion(bf16[6,128,256]{2,1,0:T(8,128)(2,1)} %get-tuple-element.14, f32[1,128,256]{2,1,0:T(8,128)} %get-tuple-element.15, bf16[1,128,256]{2,1,0:T(8,128)(2,1)S(1)} %collective-permute-done), kind=kLoop, calls=%fused_computation.1 | loop fusion | flops 131072 | bytes 262144 | tf_op jit(solution)/shard_map/dynamic_update_slice | solution.py:421
Async XLA Ops:
  89.2 6.1 %collective-permute-start = (bf16[1,128,256]{2,1,0:T(8,128)(2,1)}, bf16[1,128,256]{2,1,0:T(8,128)(2,1)S(1)}, u32[]{:S(2)}, u32[]{:S(2)}) collective-permute-start(bf16[1,128,256]{2,1,0:T(8,128)(2,1)} %get-tuple-element.16), channel_id=1, source_target_pairs={{0,1},{1,2},{2,3},{3,4},{4,5},{5,6},{6,7},{8,9},{9,10},{10,11},{11... | collective-permute-start | bytes 196616 | tf_op jit(solution)/shard_map/ppermute | solution.py:419

commit v5 on v4

--- a/solution.py
+++ b/solution.py
@@ -11,7 +11,7 @@
 CENTER = 0.5
 HALFWIDTH = 1.5
 FLOOR = 24
-DEPTH = 16
+DEPTH = 24
 CHUNKS = 4
 VMEM_BYTES = 56 * 1024 * 1024
 MESH = pl.DeviceIdType.MESH

time: 97.5 us -> 97 us (level)
  no operation moved by 1% of the time
where the time goes in v5:
time: 97 us; the launch traced here: 96.8 us
  Pallas kernels  88.3 us (91%)
  waiting for transfers between devices  5.03 us (5%)
  starting transfers between devices  1.92 us (2%)
  other arithmetic  1.55 us (2%)
    pallas_call x1, Pallas kernels, local(): pl.pallas_call(functools.partial(second_kernel, sizes), out_shape=shape(3...  40.4 us
    pallas_call x1, Pallas kernels, local(): pl.pallas_call(functools.partial(first_kernel, sizes), out_shape=shape(3...  30.8 us
    pallas_call x1, Pallas kernels, local(): pl.pallas_call(functools.partial(slots_kernel, sizes), out_shape=(shape(S...  8.75 us
    pallas_call x1, Pallas kernels, local(): pl.pallas_call(functools.partial(frame_kernel, sizes), out_shape=(shape(r...  8.3 us
    ppermute x1, waiting for transfers between devices, local(): carried = lax.ppermute(tail, 'dev', [(i, i + 1) for i in range(n_dev - 1)])  5.03 us
  transfers between devices with their start and end apart: 1, of which 1 were waited for; matrix products, arithmetic and copies ran while one was open for 0% of the time, Pallas kernels for 0%

profile of v5, /device:TPU:27, one launch (start us, length us, event | category | flops | bytes accessed | tf_op | source)
XLA Modules:
  0.0 96.8 jit_solution(12303471132407887370)
XLA Ops:
  0.0 30.8 %spread_trial.1.window.before = bf16[96,128,256]{2,1,0:T(8,128)(2,1)} custom-call(bf16[4,128,256]{2,1,0:T(8,128)(2,1)} %bitcast.2), custom_call_target="tpu_custom_call" | custom-call | tf_op jit(solution)/shard_map/spread_trial/pallas_call | solution.py:381
  30.8 8.3 %sums_first.1 = (bf16[4,128,256]{2,1,0:T(8,128)(2,1)}, f32[4,128,256]{2,1,0:T(8,128)}, bf16[5,128,256]{2,1,0:T(8,128)(2,1)}) custom-call(s32[1,33]{1,0:T(1,128)} %pointer.3, s32[1,128]{1,0:T(1,128)} %offsets.3, bf16[128,128,128]{2,1,0:T(8,128)(2,1)} %blocks.3, bf16[96,128,256]{2,1,0:T(8,128)(2,1)} %spread_trial.1.window.before), custom_call_target="tpu_custom_call" | custom-call | tf_op jit(solution)/shard_map/sums_first/pallas_call | solution.py:390
  39.1 40.4 %finish_and_spread.1.window = bf16[96,128,256]{2,1,0:T(8,128)(2,1)} custom-call(bf16[4,128,256]{2,1,0:T(8,128)(2,1)} %get-tuple-element.11.left, f32[4,128,256]{2,1,0:T(8,128)} %get-tuple-element.12.own, bf16[5,128,256]{2,1,0:T(8,128)(2,1)} %get-tuple-element.13.right, bf16[4,128,256]{2,1,0:T(8,128)(2,1)} %bitcast.3), custom_call_target="tpu_custom_call" | custom-call | tf_op jit(solution)/shard_map/finish_and_spread/pallas_call | solution.py:399
  79.5 8.8 %sums_second.1 = (bf16[6,128,256]{2,1,0:T(8,128)(2,1)}, f32[1,128,256]{2,1,0:T(8,128)}, bf16[1,128,256]{2,1,0:T(8,128)(2,1)}) custom-call(s32[1,33]{1,0:T(1,128)} %pointer.3, s32[1,128]{1,0:T(1,128)} %offsets.3, bf16[128,128,128]{2,1,0:T(8,128)(2,1)} %blocks.3, bf16[96,128,256]{2,1,0:T(8,128)(2,1)} %finish_and_spread.1.window, ...), custom_call_target="tpu_custom_call" | custom-call | tf_op jit(solution)/shard_map/sums_second/pallas_call | solution.py:408
  88.3 1.9 %collective-permute-start = (bf16[1,128,256]{2,1,0:T(8,128)(2,1)}, bf16[1,128,256]{2,1,0:T(8,128)(2,1)S(1)}, u32[]{:S(2)}, u32[]{:S(2)}) collective-permute-start(bf16[1,128,256]{2,1,0:T(8,128)(2,1)} %get-tuple-element.16), channel_id=1, source_target_pairs={{0,1},{1,2},{2,3},{3,4},{4,5},{5,6},{6,7},{8,9},{9,10},{10,11},{11... | collective-permute-start | bytes 196616 | tf_op jit(solution)/shard_map/ppermute | solution.py:419
  90.2 5.0 %collective-permute-done = bf16[1,128,256]{2,1,0:T(8,128)(2,1)S(1)} collective-permute-done((bf16[1,128,256]{2,1,0:T(8,128)(2,1)}, bf16[1,128,256]{2,1,0:T(8,128)(2,1)S(1)}, u32[]{:S(2)}, u32[]{:S(2)}) %collective-permute-start) | collective-permute-done | bytes 65568 | tf_op jit(solution)/shard_map/ppermute | solution.py:419
  95.3 1.6 %fusion = bf16[6,128,256]{2,1,0:T(8,128)(2,1)} fusion(bf16[6,128,256]{2,1,0:T(8,128)(2,1)} %get-tuple-element.14, f32[1,128,256]{2,1,0:T(8,128)} %get-tuple-element.15, bf16[1,128,256]{2,1,0:T(8,128)(2,1)S(1)} %collective-permute-done), kind=kLoop, calls=%fused_computation.1 | loop fusion | flops 131072 | bytes 262144 | tf_op jit(solution)/shard_map/dynamic_update_slice | solution.py:421
Async XLA Ops:
  88.3 7.0 %collective-permute-start = (bf16[1,128,256]{2,1,0:T(8,128)(2,1)}, bf16[1,128,256]{2,1,0:T(8,128)(2,1)S(1)}, u32[]{:S(2)}, u32[]{:S(2)}) collective-permute-start(bf16[1,128,256]{2,1,0:T(8,128)(2,1)} %get-tuple-element.16), channel_id=1, source_target_pairs={{0,1},{1,2},{2,3},{3,4},{4,5},{5,6},{6,7},{8,9},{9,10},{10,11},{11... | collective-permute-start | bytes 196616 | tf_op jit(solution)/shard_map/ppermute | solution.py:419
